TPU v7x, 512 devices: a whole 4x8x8 slice. The times are simulated.
512 devices in a mesh: section: 16 (over y_hi, x), dp: 32 (over y_lo, z, core).
Axes of the slice: x: 4, y: 8 (y_hi: 4, y_lo: 2; y = y_hi * 2 + y_lo), z: 8, core: 2. Of those that a mesh axis runs over, the one named last changes fastest.
Arguments:
- x_down: bfloat16 [32, 8, 8, 5120], P('dp'), may hold values from -6 to 6
- x_up: bfloat16 [32, 8, 8, 5120], P('dp'), may hold values from -6 to 6
- cot_down: bfloat16 [32, 8, 8, 5120], P('dp'), may hold values from -6 to 6
- cot_up: bfloat16 [32, 8, 8, 5120], P('dp'), may hold values from -6 to 6
- gain: bfloat16 [16, 5120], P('section'), may hold values from 0.25 to 1.75
- w_a: bfloat16 [16, 32, 5120], P('section'), may hold values from -0.078125 to 0.078125
- w_b: bfloat16 [16, 32, 5120], P('section'), may hold values from -1 to 1
Outputs:
- gain_gradient: float32 [16, 5120], P('section')
- grad_a: float32 [16, 32, 5120], P('section')
- grad_b: float32 [16, 32, 5120], P('section')
All inputs are finite; a program needn't handle non-finite values.
Results may differ from a plain program's by a relative error of at most 0.035.
Values may be sent and summed in bfloat16 or wider, within the bound.
A program may use at most 64 MiB of HBM per device.

v0:
```python
import jax
import jax.numpy as jnp
from jax import lax
from jax.sharding import PartitionSpec as P


def partner(value, axis, bit):
    mask = 2**bit
    pairs = [(source, source ^ mask) for source in range(lax.axis_size(axis))]
    return lax.ppermute(value, axis, pairs)


def passed_along(shard, axis, by):
    count = lax.axis_size(axis)
    pairs = [(i, i + by) for i in range(count) if 0 <= i + by < count]
    return lax.ppermute(shard, axis, pairs)


def section_forward(x, gain, w_a, w_b):
    xf = x.astype(jnp.float32)
    centered_input = xf - jnp.mean(xf, axis=-1, keepdims=True)
    inverse_deviation = lax.rsqrt(
        jnp.mean(centered_input * centered_input, axis=-1, keepdims=True) + 1e-05
    )
    standardized_input = centered_input * inverse_deviation
    normalized_output = (standardized_input * gain.astype(jnp.float32)).astype(jnp.bfloat16)
    hidden = lax.dot_general(
        normalized_output, w_a, (((1,), (1,)), ((), ())), preferred_element_type=jnp.float32
    )
    act = jax.nn.gelu(hidden).astype(jnp.bfloat16)
    return (xf + jnp.dot(act, w_b, preferred_element_type=jnp.float32)).astype(jnp.bfloat16)


def section_backward(x, grad_y, gain, w_a, w_b):
    xf = x.astype(jnp.float32)
    centered_input = xf - jnp.mean(xf, axis=-1, keepdims=True)
    inverse_deviation = lax.rsqrt(
        jnp.mean(centered_input * centered_input, axis=-1, keepdims=True) + 1e-05
    )
    standardized_input = centered_input * inverse_deviation
    gain_float = gain.astype(jnp.float32)
    normalized_output = (standardized_input * gain_float).astype(jnp.bfloat16)
    hidden = lax.dot_general(
        normalized_output, w_a, (((1,), (1,)), ((), ())), preferred_element_type=jnp.float32
    )
    act = jax.nn.gelu(hidden).astype(jnp.bfloat16)
    grad_b = lax.dot_general(
        act, grad_y, (((0,), (0,)), ((), ())), preferred_element_type=jnp.float32
    )
    grad_act = lax.dot_general(
        grad_y, w_b, (((1,), (1,)), ((), ())), preferred_element_type=jnp.float32
    )
    grad_hidden = jax.vjp(jax.nn.gelu, hidden)[1](grad_act)[0].astype(jnp.bfloat16)
    grad_a = lax.dot_general(
        grad_hidden, normalized_output, (((0,), (0,)), ((), ())), preferred_element_type=jnp.float32
    )
    normalized_gradient = jnp.dot(grad_hidden, w_a, preferred_element_type=jnp.float32)
    gain_gradient = jnp.sum(normalized_gradient * standardized_input, axis=0)
    standardized_gradient = normalized_gradient * gain_float
    inner_product = (
        standardized_gradient
        - jnp.mean(standardized_gradient, axis=-1, keepdims=True)
        - standardized_input
        * jnp.mean(standardized_gradient * standardized_input, axis=-1, keepdims=True)
    )
    grad_x = (grad_y.astype(jnp.float32) + inverse_deviation * inner_product).astype(jnp.bfloat16)
    return (grad_x, gain_gradient, grad_a, grad_b)


def pick(stack, index, count):
    return lax.dynamic_index_in_dim(stack, jnp.clip(index, 0, count - 1), 0, keepdims=False)


def place(stack, index, value, valid, count):
    slot = jnp.clip(index, 0, count - 1)
    current = lax.dynamic_index_in_dim(stack, slot, 0, keepdims=False)
    return lax.dynamic_update_index_in_dim(stack, jnp.where(valid, value, current), slot, 0)


def on_device(x_down, x_up, cot_down, cot_up, gain, w_a, w_b):
    sections = lax.axis_size("section")
    bits = sections.bit_length() - 1
    where_am = lax.axis_index("section")
    batches = x_down.shape[1]
    steps = batches + sections - 1
    own = (gain[0], w_a[0], w_b[0])
    other = own
    for bit in range(bits):
        other = partner((other[0], other[1], other[2]), "section", bit)
    inputs_down = x_down[0]
    inputs_up = x_up[0]
    first_up = sections - 1 - where_am

    def forward_step(step, carry):
        recv_down, recv_up, kept_down, kept_up = carry
        slot_down = step - where_am
        slot_up = step - first_up
        in_down = jnp.where(where_am == 0, pick(inputs_down, step, batches), recv_down)
        in_up = jnp.where(first_up == 0, pick(inputs_up, step, batches), recv_up)
        kept_down = place(
            kept_down, slot_down, in_down, (slot_down >= 0) & (slot_down < batches), batches
        )
        kept_up = place(kept_up, slot_up, in_up, (slot_up >= 0) & (slot_up < batches), batches)
        out_down = section_forward(in_down, own[0], own[1], own[2])
        out_up = section_forward(in_up, other[0], other[1], other[2])
        recv_down = passed_along(out_down, "section", 1)
        recv_up = passed_along(out_up, "section", -1)
        return (recv_down, recv_up, kept_down, kept_up)

    empty = jnp.zeros(inputs_down.shape[1:], jnp.bfloat16)
    start = (empty, empty, jnp.zeros_like(inputs_down), jnp.zeros_like(inputs_up))
    _, _, kept_down, kept_up = lax.fori_loop(0, steps, forward_step, start)
    zero_gain = jnp.zeros(own[0].shape, jnp.float32)
    zero_mat = jnp.zeros(own[1].shape, jnp.float32)
    last_down = sections - 1 - where_am

    def backward_step(step, carry):
        recv_down, recv_up, sums_down, sums_up = carry
        slot_down = step - last_down
        slot_up = step - where_am
        valid_down = (slot_down >= 0) & (slot_down < batches)
        valid_up = (slot_up >= 0) & (slot_up < batches)
        dy_down = jnp.where(where_am == sections - 1, pick(cot_down[0], step, batches), recv_down)
        dy_up = jnp.where(where_am == 0, pick(cot_up[0], step, batches), recv_up)
        dx_down, gg_down, ga_down, gb_down = section_backward(
            pick(kept_down, slot_down, batches), dy_down, own[0], own[1], own[2]
        )
        dx_up, gg_up, ga_up, gb_up = section_backward(
            pick(kept_up, slot_up, batches), dy_up, other[0], other[1], other[2]
        )
        sums_down = (
            sums_down[0] + jnp.where(valid_down, gg_down, 0.0),
            sums_down[1] + jnp.where(valid_down, ga_down, 0.0),
            sums_down[2] + jnp.where(valid_down, gb_down, 0.0),
        )
        sums_up = (
            sums_up[0] + jnp.where(valid_up, gg_up, 0.0),
            sums_up[1] + jnp.where(valid_up, ga_up, 0.0),
            sums_up[2] + jnp.where(valid_up, gb_up, 0.0),
        )
        recv_down = passed_along(dx_down, "section", -1)
        recv_up = passed_along(dx_up, "section", 1)
        return (recv_down, recv_up, sums_down, sums_up)

    zeros_three = (zero_gain, zero_mat, zero_mat)
    _, _, sums_down, sums_up = lax.fori_loop(
        0, steps, backward_step, (empty, empty, zeros_three, zeros_three)
    )
    arrived = sums_up
    for bit in range(bits):
        arrived = (
            partner(arrived[0].astype(jnp.bfloat16), "section", bit).astype(jnp.float32),
            partner(arrived[1].astype(jnp.bfloat16), "section", bit).astype(jnp.float32),
            partner(arrived[2].astype(jnp.bfloat16), "section", bit).astype(jnp.float32),
        )
    local = (sums_down[0] + arrived[0], sums_down[1] + arrived[1], sums_down[2] + arrived[2])
    total = (
        lax.psum(local[0].astype(jnp.bfloat16), "dp").astype(jnp.float32),
        lax.psum(local[1].astype(jnp.bfloat16), "dp").astype(jnp.float32),
        lax.psum(local[2].astype(jnp.bfloat16), "dp").astype(jnp.float32),
    )
    return (total[0][None], total[1][None], total[2][None])


def solution(mesh):
    placed = (
        P("dp", None, None, None),
        P("dp", None, None, None),
        P("dp", None, None, None),
        P("dp", None, None, None),
        P("section", None),
        P("section", None, None),
        P("section", None, None),
    )
    return jax.shard_map(
        on_device,
        mesh=mesh,
        in_specs=placed,
        out_specs=(P("section", None), P("section", None, None), P("section", None, None)),
        check_vma=False,
    )
```

profile of v0, /device:TPU:1, one launch (start us, length us, event | category | flops | bytes accessed | tf_op | source)
XLA Modules:
  0.0 1645.0 jit_solution(13607906056372937500)
XLA Ops:
  15.8 7.5 collective-permute-start.9
  23.4 7.0 collective-permute-start.13
  30.4 4.6 collective-permute-done.9
  46.2 14.1 collective-permute-done.10
  60.3 8.4 collective-permute-start.11
  68.8 35.3 %collective-permute-start.15 = (bf16[32,5120]{1,0:T(8,128)(2,1)S(1)}, bf16[32,5120]{1,0:T(8,128)(2,1)S(1)}, u32[]{:S(2)}, u32[]{:S(2)}) collective-permute-start(bf16[32,5120]{1,0:T(8,128)(2,1)S(1)} %collective-permute-done.14), channel_id=1, source_target_pairs={{0,256},{32,288},{64,320},{96,352},{128,384},{160,416},{192,448},{... | collective-permute-start | bytes 983048 | tf_op jit(solution)/shard_map/ppermute | solution.py:10
  122.9 6.3 collective-permute-done.7
  132.0 443.4 %while.51 = (s32[]{:T(128)}, bf16[8,5120]{1,0:T(8,128)(2,1)S(1)}, bf16[8,5120]{1,0:T(8,128)(2,1)S(1)}, bf16[8,8,5120]{2,1,0:T(8,128)(2,1)}, bf16[8,8,5120]{2,1,0...) while((s32[]{:T(128)}, bf16[8,5120]{1,0:T(8,128)(2,1)S(1)}, ...), condition=%wide.region_5.6_spmd, body=%wide.region_0.5_spmd.sunk | while | flops 11811360 | bytes 3913741 | solution.py:112
  167.4 7.2 collective-permute-start
  188.1 5.9 collective-permute-start
  207.5 5.3 collective-permute-start
  226.3 5.1 collective-permute-start
  244.8 5.3 collective-permute-start
  263.6 4.8 collective-permute-start
  281.8 5.1 collective-permute-start
  300.4 6.7 collective-permute-start
  320.5 5.6 collective-permute-start
  339.6 6.3 collective-permute-start
  359.3 6.3 collective-permute-start
  379.0 7.1 collective-permute-start
  399.6 7.1 collective-permute-start
  420.3 6.0 collective-permute-start
  431.6 4.7 collective-permute-done.1
  440.3 6.2 collective-permute-start
  460.0 7.3 collective-permute-start
  480.7 6.2 collective-permute-start
  500.4 6.5 collective-permute-start
  520.3 6.2 collective-permute-start
  540.0 6.2 collective-permute-start
  559.7 6.3 collective-permute-start
  576.7 700.0 %while.52 = (s32[]{:T(128)}, bf16[8,5120]{1,0:T(8,128)(2,1)}, bf16[8,5120]{1,0:T(8,128)(2,1)}, f32[5120]{0:T(1024)}, f32[32,5120]{1,0:T(8,128)S(1)}, /*index=5*/...) while((s32[]{:T(128)}, bf16[8,5120]{1,0:T(8,128)(2,1)}, ...), condition=%wide.region_17.18_spmd.clone, body=%wide.region_6.17_spmd.clone.sunk | while | flops 31257112 | bytes 16632213 | solution.py:146
  594.0 7.4 collective-permute-start.3
  624.3 4.6 collective-permute-start.3
  651.9 6.3 collective-permute-start.3
  681.2 7.1 collective-permute-start.3
  711.2 7.1 collective-permute-start.3
  741.2 7.1 collective-permute-start.3
  771.2 7.1 collective-permute-start.3
  801.2 7.1 collective-permute-start.3
  831.3 7.1 collective-permute-start.3
  861.3 7.1 collective-permute-start.3
  891.3 7.1 collective-permute-start.3
  921.3 7.1 collective-permute-start.3
  951.3 7.6 collective-permute-start.3
  981.8 8.3 collective-permute-start.3
  1013.1 8.3 collective-permute-start.3
  1044.3 8.3 collective-permute-start.3
  1075.5 8.3 collective-permute-start.3
  1106.7 8.3 collective-permute-start.3
  1137.9 8.3 collective-permute-start.3
  1169.1 8.3 collective-permute-start.3
  1200.4 8.3 collective-permute-start.3
  1231.6 8.3 collective-permute-start.3
  1262.8 8.3 collective-permute-start.3
  1277.9 7.0 collective-permute-start.24
  1289.3 13.6 collective-permute-start.25
  1308.0 21.3 %collective-permute-start.26 = (bf16[32,5120]{1,0:T(8,128)(2,1)S(1)}, bf16[32,5120]{1,0:T(8,128)(2,1)S(1)}, u32[]{:S(2)}, u32[]{:S(2)}) collective-permute-start(bf16[32,5120]{1,0:T(8,128)(2,1)S(1)} %collective-permute-done.25), channel_id=1, source_target_pairs={{0,128},{32,160},{64,192},{96,224},{128,0},{160,32},{192,64},{224,... | collective-permute-start | bytes 983048 | tf_op jit(solution)/shard_map/ppermute | solution.py:10
  1329.4 5.1 collective-permute-start.22
  1336.0 6.6 collective-permute-start.27
  1346.1 4.8 collective-permute-done.27
  1351.7 6.7 collective-permute-done.23
  1372.1 8.6 collective-permute-done.18
  1389.1 150.7 %psum.21 = bf16[1,5120]{1,0:T(2,128)(2,1)S(1)} all-reduce(bf16[1,5120]{1,0:T(2,128)(2,1)S(1)} %broadcast_in_dim.125), channel_id=1, replica_groups=mesh['section'=16,'dp'=32] {'dp'}, use_global_device_ids=true, to_apply=%region_18.19 | all-reduce | flops 5120 | bytes 20480 | tf_op jit(solution)/shard_map/psum | solution.py:158
  1540.4 94.9 %all-reduce.3.cloned.1.call-done = (bf16[1,32,5120]{2,1,0:T(8,128)(2,1)}, bf16[1,32,5120]{2,1,0:T(8,128)(2,1)}) async-done(((bf16[1,32,5120]{2,1,0:T(8,128)(2,1)}, bf16[1,32,5120]{2,1,0:T(8,128)(2,1)}), (bf16[1,32,5120]{2,1,0:T(8,128)(2,1)}, bf16[1,32,5120]{2,1,0:T(8,128)(2,1)})) %all-reduce.3.cloned.1.call-update) | async-done | bytes 655376 | tf_op jit(solution)/shard_map/psum | solution.py:159
  (1982 shorter events, 914.8 us)
Async XLA Ops:
  7.2 1628.2 %all-reduce.3.cloned.1.call-start = ((), (), s32[]{:S(2)}) async-start(), calls=%async_computation | async-start | bytes 1310720 | tf_op jit(solution)/shard_map/psum | solution.py:159
  11.2 12.2 collective-permute-start.12
  15.8 19.1 %collective-permute-start.9 = (bf16[32,5120]{1,0:T(8,128)(2,1)S(1)}, bf16[32,5120]{1,0:T(8,128)(2,1)S(1)}, u32[]{:S(2)}, u32[]{:S(2)}) collective-permute-start(bf16[32,5120]{1,0:T(8,128)(2,1)S(1)} %collective-permute-done.8), channel_id=1, source_target_pairs={{0,64},{32,96},{64,0},{96,32},{128,192},{160,224},{192,128},{224,1... | collective-permute-start | bytes 983048 | tf_op jit(solution)/shard_map/ppermute | solution.py:10
  23.4 18.6 %collective-permute-start.13 = (bf16[32,5120]{1,0:T(8,128)(2,1)S(1)}, bf16[32,5120]{1,0:T(8,128)(2,1)S(1)}, u32[]{:S(2)}, u32[]{:S(2)}) collective-permute-start(bf16[32,5120]{1,0:T(8,128)(2,1)S(1)} %collective-permute-done.12), channel_id=1, source_target_pairs={{0,64},{32,96},{64,0},{96,32},{128,192},{160,224},{192,128},{224,1... | collective-permute-start | bytes 983048 | tf_op jit(solution)/shard_map/ppermute | solution.py:10
  35.0 25.4 %collective-permute-start.10 = (bf16[32,5120]{1,0:T(8,128)(2,1)S(1)}, bf16[32,5120]{1,0:T(8,128)(2,1)S(1)}, u32[]{:S(2)}, u32[]{:S(2)}) collective-permute-start(bf16[32,5120]{1,0:T(8,128)(2,1)S(1)} %collective-permute-done.9), channel_id=1, source_target_pairs={{0,128},{32,160},{64,192},{96,224},{128,0},{160,32},{192,64},{224,... | collective-permute-start | bytes 983048 | tf_op jit(solution)/shard_map/ppermute | solution.py:10
  42.0 26.8 %collective-permute-start.14 = (bf16[32,5120]{1,0:T(8,128)(2,1)S(1)}, bf16[32,5120]{1,0:T(8,128)(2,1)S(1)}, u32[]{:S(2)}, u32[]{:S(2)}) collective-permute-start(bf16[32,5120]{1,0:T(8,128)(2,1)S(1)} %collective-permute-done.13), channel_id=1, source_target_pairs={{0,128},{32,160},{64,192},{96,224},{128,0},{160,32},{192,64},{224,... | collective-permute-start | bytes 983048 | tf_op jit(solution)/shard_map/ppermute | solution.py:10
  60.3 68.9 %collective-permute-start.11 = (bf16[32,5120]{1,0:T(8,128)(2,1)S(1)}, bf16[32,5120]{1,0:T(8,128)(2,1)S(1)}, u32[]{:S(2)}, u32[]{:S(2)}) collective-permute-start(bf16[32,5120]{1,0:T(8,128)(2,1)S(1)} %collective-permute-done.10), channel_id=1, source_target_pairs={{0,256},{32,288},{64,320},{96,352},{128,384},{160,416},{192,448},{... | collective-permute-start | bytes 983048 | tf_op jit(solution)/shard_map/ppermute | solution.py:10
  68.8 60.4 %collective-permute-start.15 = (bf16[32,5120]{1,0:T(8,128)(2,1)S(1)}, bf16[32,5120]{1,0:T(8,128)(2,1)S(1)}, u32[]{:S(2)}, u32[]{:S(2)}) collective-permute-start(bf16[32,5120]{1,0:T(8,128)(2,1)S(1)} %collective-permute-done.14), channel_id=1, source_target_pairs={{0,256},{32,288},{64,320},{96,352},{128,384},{160,416},{192,448},{... | collective-permute-start | bytes 983048 | tf_op jit(solution)/shard_map/ppermute | solution.py:10
  167.4 12.6 collective-permute-start
  300.4 12.1 collective-permute-start
  379.0 12.5 collective-permute-start
  399.6 12.5 collective-permute-start
  460.0 12.6 collective-permute-start
  584.7 21.8 %collective-permute-start.2 = (bf16[8,5120]{1,0:T(8,128)(2,1)}, bf16[8,5120]{1,0:T(8,128)(2,1)}, u32[]{:S(2)}, u32[]{:S(2)}) collective-permute-start(bf16[8,5120]{1,0:T(8,128)(2,1)} %fusion.228), channel_id=1, source_target_pairs={{32,0},{64,32},{96,64},{128,96},{160,128},{192,160},{224,192},{256... | collective-permute-start | bytes 245768 | tf_op jit(solution)/shard_map/while/body/eval_jaxpr/ppermute | solution.py:16
  594.0 12.5 collective-permute-start.3
  615.1 19.0 %collective-permute-start.2 = (bf16[8,5120]{1,0:T(8,128)(2,1)}, bf16[8,5120]{1,0:T(8,128)(2,1)}, u32[]{:S(2)}, u32[]{:S(2)}) collective-permute-start(bf16[8,5120]{1,0:T(8,128)(2,1)} %fusion.228), channel_id=1, source_target_pairs={{32,0},{64,32},{96,64},{128,96},{160,128},{192,160},{224,192},{256... | collective-permute-start | bytes 245768 | tf_op jit(solution)/shard_map/while/body/eval_jaxpr/ppermute | solution.py:16
  642.7 20.7 %collective-permute-start.2 = (bf16[8,5120]{1,0:T(8,128)(2,1)}, bf16[8,5120]{1,0:T(8,128)(2,1)}, u32[]{:S(2)}, u32[]{:S(2)}) collective-permute-start(bf16[8,5120]{1,0:T(8,128)(2,1)} %fusion.228), channel_id=1, source_target_pairs={{32,0},{64,32},{96,64},{128,96},{160,128},{192,160},{224,192},{256... | collective-permute-start | bytes 245768 | tf_op jit(solution)/shard_map/while/body/eval_jaxpr/ppermute | solution.py:16
  672.0 21.4 %collective-permute-start.2 = (bf16[8,5120]{1,0:T(8,128)(2,1)}, bf16[8,5120]{1,0:T(8,128)(2,1)}, u32[]{:S(2)}, u32[]{:S(2)}) collective-permute-start(bf16[8,5120]{1,0:T(8,128)(2,1)} %fusion.228), channel_id=1, source_target_pairs={{32,0},{64,32},{96,64},{128,96},{160,128},{192,160},{224,192},{256... | collective-permute-start | bytes 245768 | tf_op jit(solution)/shard_map/while/body/eval_jaxpr/ppermute | solution.py:16
  681.2 12.2 collective-permute-start.3
  702.0 21.4 %collective-permute-start.2 = (bf16[8,5120]{1,0:T(8,128)(2,1)}, bf16[8,5120]{1,0:T(8,128)(2,1)}, u32[]{:S(2)}, u32[]{:S(2)}) collective-permute-start(bf16[8,5120]{1,0:T(8,128)(2,1)} %fusion.228), channel_id=1, source_target_pairs={{32,0},{64,32},{96,64},{128,96},{160,128},{192,160},{224,192},{256... | collective-permute-start | bytes 245768 | tf_op jit(solution)/shard_map/while/body/eval_jaxpr/ppermute | solution.py:16
  711.2 12.2 collective-permute-start.3
  732.0 21.4 %collective-permute-start.2 = (bf16[8,5120]{1,0:T(8,128)(2,1)}, bf16[8,5120]{1,0:T(8,128)(2,1)}, u32[]{:S(2)}, u32[]{:S(2)}) collective-permute-start(bf16[8,5120]{1,0:T(8,128)(2,1)} %fusion.228), channel_id=1, source_target_pairs={{32,0},{64,32},{96,64},{128,96},{160,128},{192,160},{224,192},{256... | collective-permute-start | bytes 245768 | tf_op jit(solution)/shard_map/while/body/eval_jaxpr/ppermute | solution.py:16
  741.2 12.2 collective-permute-start.3
  762.0 21.4 %collective-permute-start.2 = (bf16[8,5120]{1,0:T(8,128)(2,1)}, bf16[8,5120]{1,0:T(8,128)(2,1)}, u32[]{:S(2)}, u32[]{:S(2)}) collective-permute-start(bf16[8,5120]{1,0:T(8,128)(2,1)} %fusion.228), channel_id=1, source_target_pairs={{32,0},{64,32},{96,64},{128,96},{160,128},{192,160},{224,192},{256... | collective-permute-start | bytes 245768 | tf_op jit(solution)/shard_map/while/body/eval_jaxpr/ppermute | solution.py:16
  771.2 12.2 collective-permute-start.3
  792.0 21.4 %collective-permute-start.2 = (bf16[8,5120]{1,0:T(8,128)(2,1)}, bf16[8,5120]{1,0:T(8,128)(2,1)}, u32[]{:S(2)}, u32[]{:S(2)}) collective-permute-start(bf16[8,5120]{1,0:T(8,128)(2,1)} %fusion.228), channel_id=1, source_target_pairs={{32,0},{64,32},{96,64},{128,96},{160,128},{192,160},{224,192},{256... | collective-permute-start | bytes 245768 | tf_op jit(solution)/shard_map/while/body/eval_jaxpr/ppermute | solution.py:16
  801.2 12.2 collective-permute-start.3
  822.0 21.4 %collective-permute-start.2 = (bf16[8,5120]{1,0:T(8,128)(2,1)}, bf16[8,5120]{1,0:T(8,128)(2,1)}, u32[]{:S(2)}, u32[]{:S(2)}) collective-permute-start(bf16[8,5120]{1,0:T(8,128)(2,1)} %fusion.228), channel_id=1, source_target_pairs={{32,0},{64,32},{96,64},{128,96},{160,128},{192,160},{224,192},{256... | collective-permute-start | bytes 245768 | tf_op jit(solution)/shard_map/while/body/eval_jaxpr/ppermute | solution.py:16
  831.3 12.2 collective-permute-start.3
  852.0 21.4 %collective-permute-start.2 = (bf16[8,5120]{1,0:T(8,128)(2,1)}, bf16[8,5120]{1,0:T(8,128)(2,1)}, u32[]{:S(2)}, u32[]{:S(2)}) collective-permute-start(bf16[8,5120]{1,0:T(8,128)(2,1)} %fusion.228), channel_id=1, source_target_pairs={{32,0},{64,32},{96,64},{128,96},{160,128},{192,160},{224,192},{256... | collective-permute-start | bytes 245768 | tf_op jit(solution)/shard_map/while/body/eval_jaxpr/ppermute | solution.py:16
  861.3 12.2 collective-permute-start.3
  882.0 21.4 %collective-permute-start.2 = (bf16[8,5120]{1,0:T(8,128)(2,1)}, bf16[8,5120]{1,0:T(8,128)(2,1)}, u32[]{:S(2)}, u32[]{:S(2)}) collective-permute-start(bf16[8,5120]{1,0:T(8,128)(2,1)} %fusion.228), channel_id=1, source_target_pairs={{32,0},{64,32},{96,64},{128,96},{160,128},{192,160},{224,192},{256... | collective-permute-start | bytes 245768 | tf_op jit(solution)/shard_map/while/body/eval_jaxpr/ppermute | solution.py:16
  891.3 12.2 collective-permute-start.3
  912.0 21.4 %collective-permute-start.2 = (bf16[8,5120]{1,0:T(8,128)(2,1)}, bf16[8,5120]{1,0:T(8,128)(2,1)}, u32[]{:S(2)}, u32[]{:S(2)}) collective-permute-start(bf16[8,5120]{1,0:T(8,128)(2,1)} %fusion.228), channel_id=1, source_target_pairs={{32,0},{64,32},{96,64},{128,96},{160,128},{192,160},{224,192},{256... | collective-permute-start | bytes 245768 | tf_op jit(solution)/shard_map/while/body/eval_jaxpr/ppermute | solution.py:16
  921.3 12.2 collective-permute-start.3
  942.0 22.0 %collective-permute-start.2 = (bf16[8,5120]{1,0:T(8,128)(2,1)}, bf16[8,5120]{1,0:T(8,128)(2,1)}, u32[]{:S(2)}, u32[]{:S(2)}) collective-permute-start(bf16[8,5120]{1,0:T(8,128)(2,1)} %fusion.228), channel_id=1, source_target_pairs={{32,0},{64,32},{96,64},{128,96},{160,128},{192,160},{224,192},{256... | collective-permute-start | bytes 245768 | tf_op jit(solution)/shard_map/while/body/eval_jaxpr/ppermute | solution.py:16
  951.3 12.7 collective-permute-start.3
  972.6 22.6 %collective-permute-start.2 = (bf16[8,5120]{1,0:T(8,128)(2,1)}, bf16[8,5120]{1,0:T(8,128)(2,1)}, u32[]{:S(2)}, u32[]{:S(2)}) collective-permute-start(bf16[8,5120]{1,0:T(8,128)(2,1)} %fusion.228), channel_id=1, source_target_pairs={{32,0},{64,32},{96,64},{128,96},{160,128},{192,160},{224,192},{256... | collective-permute-start | bytes 245768 | tf_op jit(solution)/shard_map/while/body/eval_jaxpr/ppermute | solution.py:16
  981.8 13.4 collective-permute-start.3
  1003.8 22.6 %collective-permute-start.2 = (bf16[8,5120]{1,0:T(8,128)(2,1)}, bf16[8,5120]{1,0:T(8,128)(2,1)}, u32[]{:S(2)}, u32[]{:S(2)}) collective-permute-start(bf16[8,5120]{1,0:T(8,128)(2,1)} %fusion.228), channel_id=1, source_target_pairs={{32,0},{64,32},{96,64},{128,96},{160,128},{192,160},{224,192},{256... | collective-permute-start | bytes 245768 | tf_op jit(solution)/shard_map/while/body/eval_jaxpr/ppermute | solution.py:16
  1013.1 13.4 collective-permute-start.3
  1035.0 22.6 %collective-permute-start.2 = (bf16[8,5120]{1,0:T(8,128)(2,1)}, bf16[8,5120]{1,0:T(8,128)(2,1)}, u32[]{:S(2)}, u32[]{:S(2)}) collective-permute-start(bf16[8,5120]{1,0:T(8,128)(2,1)} %fusion.228), channel_id=1, source_target_pairs={{32,0},{64,32},{96,64},{128,96},{160,128},{192,160},{224,192},{256... | collective-permute-start | bytes 245768 | tf_op jit(solution)/shard_map/while/body/eval_jaxpr/ppermute | solution.py:16
  1044.3 13.4 collective-permute-start.3
  1066.2 22.6 %collective-permute-start.2 = (bf16[8,5120]{1,0:T(8,128)(2,1)}, bf16[8,5120]{1,0:T(8,128)(2,1)}, u32[]{:S(2)}, u32[]{:S(2)}) collective-permute-start(bf16[8,5120]{1,0:T(8,128)(2,1)} %fusion.228), channel_id=1, source_target_pairs={{32,0},{64,32},{96,64},{128,96},{160,128},{192,160},{224,192},{256... | collective-permute-start | bytes 245768 | tf_op jit(solution)/shard_map/while/body/eval_jaxpr/ppermute | solution.py:16
  1075.5 13.4 collective-permute-start.3
  1097.5 22.6 %collective-permute-start.2 = (bf16[8,5120]{1,0:T(8,128)(2,1)}, bf16[8,5120]{1,0:T(8,128)(2,1)}, u32[]{:S(2)}, u32[]{:S(2)}) collective-permute-start(bf16[8,5120]{1,0:T(8,128)(2,1)} %fusion.228), channel_id=1, source_target_pairs={{32,0},{64,32},{96,64},{128,96},{160,128},{192,160},{224,192},{256... | collective-permute-start | bytes 245768 | tf_op jit(solution)/shard_map/while/body/eval_jaxpr/ppermute | solution.py:16
  1106.7 13.4 collective-permute-start.3
  1128.7 22.6 %collective-permute-start.2 = (bf16[8,5120]{1,0:T(8,128)(2,1)}, bf16[8,5120]{1,0:T(8,128)(2,1)}, u32[]{:S(2)}, u32[]{:S(2)}) collective-permute-start(bf16[8,5120]{1,0:T(8,128)(2,1)} %fusion.228), channel_id=1, source_target_pairs={{32,0},{64,32},{96,64},{128,96},{160,128},{192,160},{224,192},{256... | collective-permute-start | bytes 245768 | tf_op jit(solution)/shard_map/while/body/eval_jaxpr/ppermute | solution.py:16
  1137.9 13.4 collective-permute-start.3
  1159.9 22.6 %collective-permute-start.2 = (bf16[8,5120]{1,0:T(8,128)(2,1)}, bf16[8,5120]{1,0:T(8,128)(2,1)}, u32[]{:S(2)}, u32[]{:S(2)}) collective-permute-start(bf16[8,5120]{1,0:T(8,128)(2,1)} %fusion.228), channel_id=1, source_target_pairs={{32,0},{64,32},{96,64},{128,96},{160,128},{192,160},{224,192},{256... | collective-permute-start | bytes 245768 | tf_op jit(solution)/shard_map/while/body/eval_jaxpr/ppermute | solution.py:16
  1169.1 13.4 collective-permute-start.3
  1191.1 22.6 %collective-permute-start.2 = (bf16[8,5120]{1,0:T(8,128)(2,1)}, bf16[8,5120]{1,0:T(8,128)(2,1)}, u32[]{:S(2)}, u32[]{:S(2)}) collective-permute-start(bf16[8,5120]{1,0:T(8,128)(2,1)} %fusion.228), channel_id=1, source_target_pairs={{32,0},{64,32},{96,64},{128,96},{160,128},{192,160},{224,192},{256... | collective-permute-start | bytes 245768 | tf_op jit(solution)/shard_map/while/body/eval_jaxpr/ppermute | solution.py:16
  1200.4 13.4 collective-permute-start.3
  1222.3 22.6 %collective-permute-start.2 = (bf16[8,5120]{1,0:T(8,128)(2,1)}, bf16[8,5120]{1,0:T(8,128)(2,1)}, u32[]{:S(2)}, u32[]{:S(2)}) collective-permute-start(bf16[8,5120]{1,0:T(8,128)(2,1)} %fusion.228), channel_id=1, source_target_pairs={{32,0},{64,32},{96,64},{128,96},{160,128},{192,160},{224,192},{256... | collective-permute-start | bytes 245768 | tf_op jit(solution)/shard_map/while/body/eval_jaxpr/ppermute | solution.py:16
  1231.6 13.4 collective-permute-start.3
  1253.5 22.6 %collective-permute-start.2 = (bf16[8,5120]{1,0:T(8,128)(2,1)}, bf16[8,5120]{1,0:T(8,128)(2,1)}, u32[]{:S(2)}, u32[]{:S(2)}) collective-permute-start(bf16[8,5120]{1,0:T(8,128)(2,1)} %fusion.228), channel_id=1, source_target_pairs={{32,0},{64,32},{96,64},{128,96},{160,128},{192,160},{224,192},{256... | collective-permute-start | bytes 245768 | tf_op jit(solution)/shard_map/while/body/eval_jaxpr/ppermute | solution.py:16
  1262.8 13.4 collective-permute-start.3
  1284.9 18.0 %collective-permute-start.20 = (bf16[32,5120]{1,0:T(8,128)(2,1)S(1)}, bf16[32,5120]{1,0:T(8,128)(2,1)S(1)}, u32[]{:S(2)}, u32[]{:S(2)}) collective-permute-start(bf16[32,5120]{1,0:T(8,128)(2,1)S(1)} %convert_element_type.307), channel_id=1, source_target_pairs={{0,32},{32,0},{64,96},{96,64},{128,160},{160,128},{192,224},{224,1... | collective-permute-start | bytes 983048 | tf_op jit(solution)/shard_map/ppermute | solution.py:10
  1289.3 18.7 %collective-permute-start.25 = (bf16[32,5120]{1,0:T(8,128)(2,1)S(1)}, bf16[32,5120]{1,0:T(8,128)(2,1)S(1)}, u32[]{:S(2)}, u32[]{:S(2)}) collective-permute-start(bf16[32,5120]{1,0:T(8,128)(2,1)S(1)} %collective-permute-done.24), channel_id=1, source_target_pairs={{0,64},{32,96},{64,0},{96,32},{128,192},{160,224},{192,128},{224,1... | collective-permute-start | bytes 983048 | tf_op jit(solution)/shard_map/ppermute | solution.py:10
  1302.9 26.4 %collective-permute-start.21 = (bf16[32,5120]{1,0:T(8,128)(2,1)S(1)}, bf16[32,5120]{1,0:T(8,128)(2,1)S(1)}, u32[]{:S(2)}, u32[]{:S(2)}) collective-permute-start(bf16[32,5120]{1,0:T(8,128)(2,1)S(1)} %collective-permute-done.20), channel_id=1, source_target_pairs={{0,64},{32,96},{64,0},{96,32},{128,192},{160,224},{192,128},{224,1... | collective-permute-start | bytes 983048 | tf_op jit(solution)/shard_map/ppermute | solution.py:10
  1308.0 27.9 %collective-permute-start.26 = (bf16[32,5120]{1,0:T(8,128)(2,1)S(1)}, bf16[32,5120]{1,0:T(8,128)(2,1)S(1)}, u32[]{:S(2)}, u32[]{:S(2)}) collective-permute-start(bf16[32,5120]{1,0:T(8,128)(2,1)S(1)} %collective-permute-done.25), channel_id=1, source_target_pairs={{0,128},{32,160},{64,192},{96,224},{128,0},{160,32},{192,64},{224,... | collective-permute-start | bytes 983048 | tf_op jit(solution)/shard_map/ppermute | solution.py:10
  1329.4 13.3 collective-permute-start.22
  1336.0 14.9 collective-permute-start.27
  1342.6 15.8 collective-permute-start.23
  (451 other events, 1270.6 us)
Sparse Core Ops, SparseCore 0:
  1359.3 275.9 all-reduce.2
where the time goes:
time: 1670 us; the launch traced here: 1640 us
  starting transfers between devices  520 us (31%)
  other arithmetic  316 us (19%)
  matrix products  272 us (16%)
  waiting for transfers between devices  263 us (16%)
  blocking collectives  151 us (9%)
  local copies, waits for them, and re-layouts  100 us (6%)
    ppermute x92, starting transfers between devices, passed_along(): return lax.ppermute(shard, axis, pairs)  364 us
    ppermute x24, starting transfers between devices, partner(): return lax.ppermute(value, axis, pairs)  156 us
    psum x1, blocking collectives, on_device(): lax.psum(local[0].astype(jnp.bfloat16), 'dp').astype(jnp.float32)  151 us
    psum x1, waiting for transfers between devices, on_device(): lax.psum(local[1].astype(jnp.bfloat16), 'dp').astype(jnp.float32)  94.9 us
    ppermute x92, waiting for transfers between devices, passed_along(): return lax.ppermute(shard, axis, pairs)  94.8 us
    dot_general x46, matrix products, section_backward(): lax.dot_general(normalized_output, w_a, (((1,), (1,)), ((), ())), preferr...  80.8 us
    convert_element_type x46, other arithmetic, section_backward(): (grad_y.astype(jnp.float32) + inverse_deviation * inner_product).astype(j...  75.7 us
    ppermute x24, waiting for transfers between devices, partner(): return lax.ppermute(value, axis, pairs)  73.7 us
  transfers between devices with their start and end apart: 117, of which 41 were waited for; matrix products, arithmetic and copies ran while one was open for 21% of the time, Pallas kernels for 0%

commit v1 on v0

v1 whole, which is shorter than its diff:
```python
import jax
import jax.numpy as jnp
from jax import lax
from jax.experimental import pallas as pl
from jax.experimental.pallas import tpu as pltpu
from jax.sharding import PartitionSpec as P

F32, BF16 = jnp.float32, jnp.bfloat16
S, R, H, LANES = 16, 32, 16, 512
MBS = 8
MESH = pl.DeviceIdType.MESH
NT = (((1,), (1,)), ((), ()))
TN = (((0,), (0,)), ((), ()))


def dot(a, b, dims=(((1,), (0,)), ((), ()))):
    return lax.dot_general(a, b, dims, preferred_element_type=F32)


def gelu_pair(h):
    k = 0.7978845608028654
    t = jnp.tanh(k * (h + 0.044715 * h * h * h))
    act = 0.5 * h * (1.0 + t)
    slope = 0.5 * (1.0 + t) + 0.5 * h * (1.0 - t * t) * (k * (1.0 + 3 * 0.044715 * h * h))
    return act, slope


def halves(m):
    hi = m.astype(BF16)
    return hi, (m - hi.astype(F32)).astype(BF16)


def chain_kernel(rows_ref, w_ref, msg_ref, sc_ref, mn, kt, raw):
    width = rows_ref.shape[1]
    gw_ref, wb_ref = w_ref.at[0:LANES], w_ref.at[LANES:]
    def block(b, _):
        cols = pl.ds(pl.multiple_of(b * 256, 256), 256)
        raw[b] = dot(wb_ref[...], gw_ref[cols, :], NT)
        raw[b + 2] = dot(wb_ref[...], wb_ref[cols, :], NT)
        return 0
    lax.fori_loop(0, 2, block, 0)
    for b in range(4):
        for s in range(S):
            part = raw[b, s * R:(s + 1) * R, :]
            hi, lo = halves(part)
            mn[s, 0:R, b * 256:(b + 1) * 256] = hi
            mn[s, R:2 * R, b * 256:(b + 1) * 256] = lo
    for b in range(2):
        for t in range(4):
            for u in range(2):
                tile = raw[b, t * 128:(t + 1) * 128, u * 128:(u + 1) * 128].T
                hi, lo = halves(tile)
                for q in range(4):
                    s = (b * 2 + u) * 4 + q
                    kt[s, 0:R, t * 128:(t + 1) * 128] = hi[q * R:(q + 1) * R]
                    kt[s, R:2 * R, t * 128:(t + 1) * 128] = lo[q * R:(q + 1) * R]
    rows = rows_ref[...]
    x0 = rows[0:8].astype(F32)
    lhs = jnp.concatenate([rows, jnp.ones_like(rows)], axis=0)
    pg = dot(lhs, gw_ref[...], NT)
    pb = dot(lhs, wb_ref[...], NT)
    u, v, c = pg[0:8], pb[0:8], pb[8:16]
    gws, wbs = pg[16:17], pb[16:17]
    mu = jnp.sum(x0, axis=1, keepdims=True) / width
    cen = x0 - mu
    q = jnp.sum(cen * cen, axis=1, keepdims=True)
    lane = lax.broadcasted_iota(jnp.int32, (8, LANES), 1)
    hid, slope, rstds, mus, vs, acts = [], [], [], [], [], []
    for s in range(S):
        sl = slice(s * R, (s + 1) * R)
        rstd = lax.rsqrt(q / width + 1e-5)
        h = rstd * (u[:, sl] - mu * gws[:, sl])
        a, g = gelu_pair(h)
        a16 = a.astype(BF16)
        af = a16.astype(F32)
        hid.append(h); slope.append(g); rstds.append(rstd); mus.append(mu); vs.append(v); acts.append(af)
        if s < S - 1:
            step = dot(jnp.concatenate([a16, a16], axis=1), mn[s])
            v_new = v + step[:, LANES:]
            u = u + step[:, :LANES]
            tot = jnp.sum(af * wbs[:, sl], axis=1, keepdims=True)
            q = q + jnp.sum(af * (v[:, sl] + v_new[:, sl] - (2.0 * mu) * wbs[:, sl]), axis=1, keepdims=True) - tot * tot / width
            q = jnp.maximum(q, 0.0)
            mu = mu + tot / width
            v = v_new
    fs, cs, es = [None] * S, [None] * S, [None] * S
    cc = jnp.zeros_like(mu)
    ee = jnp.zeros_like(mu)
    for j in range(S - 1, -1, -1):
        sl = slice(j * R, (j + 1) * R)
        cs[j], es[j] = cc, ee
        dh = (c[:, sl] * slope[j]).astype(BF16)
        dhf = dh.astype(F32)
        rstd = rstds[j]
        a_j = rstd * jnp.sum(dhf * gws[:, sl], axis=1, keepdims=True) / width
        c_j = rstd * rstd * jnp.sum(dhf * hid[j], axis=1, keepdims=True) / width
        e_j = a_j - c_j * mus[j]
        fs[j] = rstd * dhf
        if j > 0:
            step = dot(jnp.concatenate([dh, dh], axis=1), kt[j])
            c = c + rstd * step - c_j * vs[j] - e_j * wbs
        cc = cc + c_j
        ee = ee + e_j
    act_all = jnp.concatenate(acts, axis=1)
    d_all = jnp.concatenate([acts[i] * cs[i] for i in range(S - 1)] + [acts[S - 1]], axis=1)
    f_all = jnp.concatenate(fs, axis=1)
    lane_sc = lax.broadcasted_iota(jnp.int32, (8, 128), 1)
    for s in range(S):
        z = jnp.where(lane < s * R, act_all, d_all)
        z = jnp.concatenate([z[:, :LANES - R], acts[s]], axis=1)
        f = jnp.concatenate([fs[s], f_all[:, R:]], axis=1)
        msg_ref[s] = jnp.concatenate([z, f], axis=0).astype(BF16)
        sc_ref[s] = jnp.where(lane_sc == 0, mus[s], jnp.where(lane_sc == 1, cs[s], es[s]))


def chain(rows, w):
    width = rows.shape[1]
    return pl.pallas_call(
        chain_kernel,
        out_shape=(jax.ShapeDtypeStruct((S, 16, LANES), BF16), jax.ShapeDtypeStruct((S, 8, 128), F32)),
        in_specs=[pl.BlockSpec(memory_space=pltpu.VMEM)] * 2,
        out_specs=(pl.BlockSpec(memory_space=pltpu.VMEM),) * 2,
        scratch_shapes=[
            pltpu.VMEM((S, 2 * R, 2 * LANES), BF16),
            pltpu.VMEM((S, 2 * R, LANES), BF16),
            pltpu.VMEM((4, LANES, 256), F32),
        ],
        compiler_params=pltpu.CompilerParams(vmem_limit_bytes=56 * 2**20),
    )(rows, w)


def final_kernel(msg_ref, sc_ref, xd, xu, cd, cu, w_ref, out_ref):
    gw_ref, wb_ref = w_ref.at[0:LANES], w_ref.at[LANES:]
    s = lax.axis_index("section")
    z = jnp.concatenate([msg_ref[i, 0:8] for i in range(S)], axis=0)
    f = jnp.concatenate([msg_ref[i, 8:16] for i in range(S)], axis=0)
    sc = jnp.concatenate([sc_ref[i] for i in range(S)], axis=0)
    mu, cc, ee = sc[:, 0:1], sc[:, 1:2], sc[:, 2:3]
    lane = lax.broadcasted_iota(jnp.int32, z.shape, 1)
    zero = jnp.zeros_like(z)
    zx = jnp.where(lane < s * R, z, zero)
    zd = jnp.where((lane >= s * R) & (lane < LANES - R), z, zero)
    fd = jnp.where(lane >= (s + 1) * R, f, zero)
    act, fs = z[:, LANES - R:], f[:, :R]
    x = jnp.concatenate([xd[...], xu[...]], axis=0).astype(F32) + dot(zx, wb_ref[...])
    dy = jnp.concatenate([cd[...], cu[...]], axis=0).astype(F32) + dot(fd, gw_ref[...]) - dot(zd, wb_ref[...])
    dy = dy - cc * x - ee
    out_ref[0, 0:R] = dot(fs, (x - mu).astype(BF16), TN).astype(BF16)
    out_ref[0, R:2 * R] = dot(act, dy.astype(BF16), TN).astype(BF16)


def final(msg, sc, xd, xu, cd, cu, w, step=640):
    width = xd.shape[1]
    n = width // step
    col = lambda rows: pl.BlockSpec((rows, step), lambda i: (0, i))
    whole = lambda shape: pl.BlockSpec(shape, lambda i: (0,) * len(shape))
    return pl.pallas_call(
        final_kernel,
        grid=(n,),
        out_shape=jax.ShapeDtypeStruct((n, 2 * R, step), BF16),
        in_specs=[whole(msg.shape), whole(sc.shape)] + [col(xd.shape[0])] * 4 + [col(w.shape[0])],
        out_specs=pl.BlockSpec((1, 2 * R, step), lambda i: (i, 0, 0)),
        compiler_params=pltpu.CompilerParams(vmem_limit_bytes=56 * 2**20),
    )(msg, sc, xd, xu, cd, cu, w)


def place():
    me, dp = lax.axis_index("section"), lax.axis_index("dp")
    deep = lax.axis_size("dp") // 4
    core = lax.rem(dp, 2)
    z = lax.rem(dp // 2, deep)
    y_lo = dp // (2 * deep)
    return me, me // 4, lax.rem(me, 4), y_lo, z, core, deep


def greet(partners):
    barrier = pltpu.get_barrier_semaphore()
    for partner in partners:
        pl.semaphore_signal(barrier, inc=1, device_id=partner, device_id_type=MESH)
    pl.semaphore_wait(barrier, len(partners))


class Units:
    def __init__(self, buf, send, recv):
        self.buf, self.send, self.recv = buf, send, recv
        self.pending = []
        self.next = 0

    def view(self, kind, sec, half):
        return self.buf.at[kind, sec, pl.ds(pl.multiple_of(half * H, H), H)]

    def copy(self, kind, sec, half, slot, to, index):
        return pltpu.make_async_remote_copy(
            src_ref=self.view(kind, sec, half), dst_ref=self.view(kind, sec, half),
            send_sem=self.send.at[index], recv_sem=self.recv.at[slot], device_id=to, device_id_type=MESH)

    def push(self, kind, sec, half, slot, to):
        c = self.copy(kind, sec, half, slot, to, self.next)
        c.start()
        self.pending.append(c)
        self.next += 1

    def arrived(self, kind, sec, half, slot, to):
        self.copy(kind, sec, half, slot, to, 0).wait_recv()

    def drain(self):
        for c in self.pending:
            c.wait_send()


def spread(buf, send, recv, after=lambda *a: None):
    me, p, x, y_lo, z, core, deep = place()
    dp = lax.axis_index("dp")
    sgn = 2 * y_lo - 1
    row = lambda d: lax.rem(p + d + 4, 4)
    col = lambda d: lax.rem(x + d + 4, 4)
    other_y = dp + (1 - 2 * y_lo) * (2 * deep)
    right, left = (p * 4 + col(1), dp), (p * 4 + col(-1), dp)
    cross = (row(sgn) * 4 + x, other_y)
    pair = (me, other_y)
    sib = (me, dp + 1 - 2 * core)
    greet([right, left, cross, pair, sib])
    SIB = 32

    def run(kind):
        un = Units(buf, send, recv)
        push, got = un.push, un.arrived
        n_sib = [0]

        def share(sec, half):
            push(kind, sec, half, SIB + n_sib[0], sib)
            n_sib[0] += 1

        def x1(r, base):
            sec = r * 4 + x
            push(kind, sec, 0, base + 0, right)
            push(kind, sec, 1, base + 3, left)
            push(kind, sec, 1, base + 1, right)
            push(kind, sec, 0, base + 2, left)

        def y1(t, half, base):
            push(kind, p * 4 + t, half, base + half, cross)

        def x_wait(r, base, which, then=None):
            d, half, who = [(-1, 0, right), (-1, 1, right), (1, 0, left), (1, 1, left), (2, 0, right), (2, 1, left)][which]
            sec = r * 4 + col(d)
            got(kind, sec, half, base + which, who)
            if which == 0:
                push(kind, sec, 0, base + 4, right)
            if which == 3:
                push(kind, sec, 1, base + 5, left)
            if then is not None:
                then(col(d), half)
            share(sec, half)
            after(kind, sec, half)

        def y_wait(t, base, which, then=None):
            if which < 2:
                sec, half, who = row(sgn) * 4 + t, which, cross
            elif which < 4:
                sec, half, who = row(-sgn) * 4 + t, which - 2, pair
            elif which == 4:
                sec, half, who = row(2) * 4 + t, 1 - y_lo, cross
            else:
                sec, half, who = row(2) * 4 + t, y_lo, pair
            got(kind, sec, half, base + which, who)
            if which < 2:
                push(kind, sec, half, base + 2 + which, pair)
            if which == 3:
                push(kind, sec, y_lo, base + 4, cross)
            if which == 4:
                push(kind, sec, half, base + 5, pair)
            if then is not None:
                then(sec // 4, half)
            share(sec, half)
            after(kind, sec, half)

        return un, share, x1, y1, x_wait, y_wait

    def core0():
        un, share, x1, y1, x_wait, y_wait = run(0)
        B = [6, 12, 18, 24]
        x1(p, 0)
        y1(x, 0, B[0]); y1(x, 1, B[0])
        share(me, 0); share(me, 1)
        x_wait(p, 0, 0, lambda t, h: y1(t, h, B[1]))
        x_wait(p, 0, 3, lambda t, h: y1(t, h, B[2]))
        x_wait(p, 0, 1, lambda t, h: y1(t, h, B[1]))
        x_wait(p, 0, 2, lambda t, h: y1(t, h, B[2]))
        y_wait(x, B[0], 0)
        y_wait(x, B[0], 1)
        x_wait(p, 0, 4, lambda t, h: y1(t, h, B[3]))
        x_wait(p, 0, 5, lambda t, h: y1(t, h, B[3]))
        y_wait(x, B[0], 2)
        y_wait(x, B[0], 3)
        ts = [x, col(-1), col(1), col(2)]
        for i in (1, 2, 3):
            for w in (0, 1, 2, 3):
                y_wait(ts[i], B[i], w)
        for i in range(4):
            y_wait(ts[i], B[i], 4)
        for i in range(4):
            y_wait(ts[i], B[i], 5)
        un.drain()

    def core1():
        un, share, x1, y1, x_wait, y_wait = run(1)
        B = [6, 12, 18, 24]
        y1(x, 0, 0); y1(x, 1, 0)
        x1(p, B[0])
        share(me, 0); share(me, 1)
        y_wait(x, 0, 0)
        y_wait(x, 0, 1)
        x1(row(sgn), B[1])
        x_wait(p, B[0], 0)
        x_wait(p, B[0], 3)
        y_wait(x, 0, 2)
        y_wait(x, 0, 3)
        x1(row(-sgn), B[2])
        x_wait(p, B[0], 1)
        x_wait(p, B[0], 2)
        y_wait(x, 0, 4)
        y_wait(x, 0, 5)
        x1(row(2), B[3])
        x_wait(p, B[0], 4)
        x_wait(p, B[0], 5)
        for i, r in ((1, row(sgn)), (2, row(-sgn)), (3, row(2))):
            for w in (0, 3, 1, 2):
                x_wait(r, B[i], w)
        for i, r in ((1, row(sgn)), (2, row(-sgn)), (3, row(2))):
            for w in (4, 5):
                x_wait(r, B[i], w)
        un.drain()

    pl.when(core == 0)(core0)
    pl.when(core == 1)(core1)
    def take(kind, secs):
        un = Units(buf, send, recv)
        for i, (sec, half) in enumerate(secs):
            un.arrived(kind, sec, half, SIB + i, sib)
            after(kind, sec, half)

    far = row(2)
    def order0():
        ts = [x, col(-1), col(1), col(2)]
        o = [(me, 0), (me, 1), (p * 4 + col(-1), 0), (p * 4 + col(1), 1), (p * 4 + col(-1), 1), (p * 4 + col(1), 0)]
        a, b = row(sgn), row(-sgn)
        o += [(a * 4 + x, 0), (a * 4 + x, 1), (p * 4 + col(2), 0), (p * 4 + col(2), 1), (b * 4 + x, 0), (b * 4 + x, 1)]
        for i in (1, 2, 3):
            o += [(a * 4 + ts[i], 0), (a * 4 + ts[i], 1), (b * 4 + ts[i], 0), (b * 4 + ts[i], 1)]
        o += [(far * 4 + t, 1 - y_lo) for t in ts] + [(far * 4 + t, y_lo) for t in ts]
        return o

    def order1():
        a, b = row(sgn), row(-sgn)
        k = lambda r, w: [(r * 4 + col(-1), 0), (r * 4 + col(-1), 1), (r * 4 + col(1), 0), (r * 4 + col(1), 1), (r * 4 + col(2), 0), (r * 4 + col(2), 1)][w]
        o = [(me, 0), (me, 1), (a * 4 + x, 0), (a * 4 + x, 1), k(p, 0), k(p, 3), (b * 4 + x, 0), (b * 4 + x, 1), k(p, 1), k(p, 2),
             (far * 4 + x, 1 - y_lo), (far * 4 + x, y_lo), k(p, 4), k(p, 5)]
        for r in (a, b, far):
            o += [k(r, w) for w in (0, 3, 1, 2)]
        for r in (a, b, far):
            o += [k(r, w) for w in (4, 5)]
        return o

    pl.when(core == 1)(lambda: take(0, order0()))
    pl.when(core == 0)(lambda: take(1, order1()))


def gather_kernel(own_ref, all_ref, send, recv, local):
    me, core = lax.axis_index("section"), lax.rem(lax.axis_index("dp"), 2)
    for kind in range(2):
        c = pltpu.make_async_copy(own_ref.at[kind], all_ref.at[kind, me], local.at[kind])
        pl.when(core == kind)(c.start)
        pl.when(core == kind)(c.wait)
    spread(all_ref, send, recv)


def gather(own, collective_id=1):
    return pl.pallas_call(
        gather_kernel,
        out_shape=jax.ShapeDtypeStruct((2, S) + own.shape[1:], BF16),
        in_specs=[pl.BlockSpec(memory_space=pl.ANY)],
        out_specs=pl.BlockSpec(memory_space=pl.ANY),
        scratch_shapes=[pltpu.SemaphoreType.DMA((64,)), pltpu.SemaphoreType.DMA((64,)), pltpu.SemaphoreType.DMA((2,))],
        compiler_params=pltpu.CompilerParams(collective_id=collective_id, has_side_effects=True),
    )(own)


def swap_kernel(msg_ref, sc_ref, msg_out, sc_out, send, recv, local):
    me, dp = lax.axis_index("section"), lax.axis_index("dp")
    ids = [lax.rem(me + d, S) for d in range(1, S)]
    greet([(i, dp) for i in ids])
    own = [pltpu.make_async_copy(msg_ref.at[me], msg_out.at[me], local.at[0]), pltpu.make_async_copy(sc_ref.at[me], sc_out.at[me], local.at[1])]
    out = []
    for d, i in enumerate(ids):
        for k, (a, b) in enumerate(((msg_ref, msg_out), (sc_ref, sc_out))):
            out.append(pltpu.make_async_remote_copy(
                src_ref=a.at[i], dst_ref=b.at[me], send_sem=send.at[k, d], recv_sem=recv.at[k, d], device_id=(i, dp), device_id_type=MESH))
    for c in out + own:
        c.start()
    for c in out + own:
        c.wait()


def swap(msg, sc, collective_id=2):
    return pl.pallas_call(
        swap_kernel,
        out_shape=(jax.ShapeDtypeStruct(msg.shape, msg.dtype), jax.ShapeDtypeStruct(sc.shape, sc.dtype)),
        in_specs=[pl.BlockSpec(memory_space=pltpu.VMEM)] * 2,
        out_specs=(pl.BlockSpec(memory_space=pltpu.VMEM),) * 2,
        scratch_shapes=[pltpu.SemaphoreType.DMA((2, S)), pltpu.SemaphoreType.DMA((2, S)), pltpu.SemaphoreType.DMA((2,))],
        compiler_params=pltpu.CompilerParams(collective_id=collective_id, has_side_effects=True),
    )(msg, sc)


def reduce_kernel(g_ref, out_ref, near, part, pieces, total, send, recv):
    me, p, x, y_lo, z, core, deep = place()
    dp = lax.axis_index("dp")
    n = 2 * deep
    sib = (me, dp + 1 - 2 * core)
    mine = y_lo * deep + z
    spots = [lax.rem(mine + d, n) for d in range(1, n)]
    ids = [(me, q * 2 + core) for q in spots]
    greet([sib] + ids)
    theirs = 1 - core
    c = pltpu.make_async_remote_copy(
        src_ref=g_ref.at[:, pl.ds(pl.multiple_of(theirs * R, R), R)], dst_ref=near,
        send_sem=send.at[0], recv_sem=recv.at[0], device_id=sib, device_id_type=MESH)
    c.start()
    c.wait()
    for i in range(deep):
        part[i] = (near[i].astype(F32) + g_ref[i, pl.ds(pl.multiple_of(core * R, R), R)].astype(F32)).astype(BF16)

    def piece(q):
        return part.at[lax.rem(q, deep), pl.ds(pl.multiple_of((q // deep) * H, H), H)]
    out = []
    for d, q in enumerate(spots):
        out.append(pltpu.make_async_remote_copy(
            src_ref=piece(q), dst_ref=pieces.at[d], send_sem=send.at[1 + d], recv_sem=recv.at[1 + d], device_id=ids[d], device_id_type=MESH))
        out[-1].start()
    acc = piece(mine)[...].astype(F32)
    for d, cpy in enumerate(out):
        cpy.wait_recv()
        acc = acc + pieces[d].astype(F32)
    total[...] = acc.astype(BF16)
    back = []
    for d, q in enumerate(spots):
        back.append(pltpu.make_async_remote_copy(
            src_ref=total, dst_ref=out_ref.at[core, mine], send_sem=send.at[n + d], recv_sem=recv.at[n + d], device_id=ids[d], device_id_type=MESH))
        back[-1].start()
    out_ref[core, mine] = total[...]
    hand = []

    def share(kind, spot, slot):
        return pltpu.make_async_remote_copy(
            src_ref=out_ref.at[kind, spot], dst_ref=out_ref.at[kind, spot], send_sem=send.at[2 * n + slot], recv_sem=recv.at[2 * n + slot],
            device_id=sib, device_id_type=MESH)
    hand.append(share(core, mine, 0))
    hand[-1].start()
    for d in range(n - 1):
        src = lax.rem(mine + n - 1 - d, n)
        pltpu.make_async_remote_copy(
            src_ref=total, dst_ref=out_ref.at[core, src], send_sem=send.at[n + d], recv_sem=recv.at[n + d], device_id=ids[d], device_id_type=MESH).wait_recv()
        hand.append(share(core, src, 1 + d))
        hand[-1].start()
    for d in range(n):
        src = lax.rem(mine + n - d, n)
        share(theirs, src, d).wait_recv()
    for cpy in out + back + hand:
        cpy.wait_send()


def reduce(g, collective_id=3):
    deep, _, cols = g.shape
    n = 2 * deep
    return pl.pallas_call(
        reduce_kernel,
        out_shape=jax.ShapeDtypeStruct((2, n, H, cols), BF16),
        in_specs=[pl.BlockSpec(memory_space=pltpu.VMEM)],
        out_specs=pl.BlockSpec(memory_space=pltpu.VMEM),
        scratch_shapes=[
            pltpu.VMEM((deep, R, cols), BF16), pltpu.VMEM((deep, R, cols), BF16), pltpu.VMEM((n, H, cols), BF16), pltpu.VMEM((H, cols), BF16),
            pltpu.SemaphoreType.DMA((3 * n + 1,)), pltpu.SemaphoreType.DMA((3 * n + 1,))],
        compiler_params=pltpu.CompilerParams(collective_id=collective_id, has_side_effects=True, vmem_limit_bytes=40 * 2**20),
    )(g)


def on_device(x_down, x_up, cot_down, cot_up, gain, w_a, w_b):
    width = x_down.shape[-1]
    me = lax.axis_index("section")
    rows = MBS * 8
    xd, xu, cd, cu = [t.reshape(rows, width) for t in (x_down, x_up, cot_down, cot_up)]
    gf, wa = gain[0].astype(F32), w_a[0].astype(F32)
    own = jnp.stack([(gf * wa).astype(BF16), w_b[0]])
    w = gather(own).reshape(2 * LANES, width)

    def mine(down, up):
        at = lax.rem(me, MBS) * 8
        return jnp.where(me < MBS, lax.dynamic_slice_in_dim(down, at, 8), lax.dynamic_slice_in_dim(up, at, 8))

    picked = jnp.concatenate([mine(xd, xu), mine(cd, cu)], axis=0)
    msg, sc = swap(*chain(picked, w))
    partial = final(msg, sc, xd, xu, cd, cu, w)
    total = reduce(partial)
    deep, cols = partial.shape[0], partial.shape[2]
    total = total.reshape(2, 2, deep, H, cols).transpose(0, 1, 3, 2, 4).reshape(2, R, width).astype(F32)
    return ((wa * total[0]).sum(0)[None], (gf * total[0])[None], total[1][None])


def solution(mesh):
    data, held = P("dp", None, None, None), P("section", None, None)
    return jax.shard_map(
        on_device,
        mesh=mesh,
        in_specs=(data, data, data, data, P("section", None), held, held),
        out_specs=(P("section", None), held, held),
        check_vma=False,
    )
```

time: 1670 us -> 162 us (0.10); the launches traced: 1640 us -> 161 us
  starting transfers between devices: 520 us -> 0 us
  other arithmetic: 316 us -> 6.15 us
  matrix products: 272 us -> 0 us
  waiting for transfers between devices: 263 us -> 0 us
  Pallas kernels: 0 us -> 151 us
  blocking collectives: 151 us -> 0 us
  local copies, waits for them, and re-layouts: 100 us -> 3.41 us
    ppermute x116 -> x0, starting transfers between devices: 520 us -> none  [the longest x92 364 us: passed_along(): return lax.ppermute(shard, axis, pairs)]
    dot_general x276 -> x0, matrix products: 272 us -> none  [the longest x46 80.8 us: section_backward(): lax.dot_general(normalized_output, w_a, (((1,), (1,)), ((), ())), preferr...]
    ppermute x116 -> x0, waiting for transfers between devices: 169 us -> none  [the longest x92 94.8 us: passed_along(): return lax.ppermute(shard, axis, pairs)]
    pallas_call x0 -> x5, Pallas kernels: none -> 151 us  [the longest x1 64.9 us: gather(): pl.pallas_call(gather_kernel, out_shape=jax.ShapeDtypeStruct((2, S) + own...]
    psum x1 -> x0, blocking collectives: 151 us -> none  [on_device(): lax.psum(local[0].astype(jnp.bfloat16), 'dp').astype(jnp.float32)]
    reduce_sum x184 -> x1, other arithmetic: 117 us -> 0.71 us  [on_device(): return ((wa * total[0]).sum(0)[None], (gf * total[0])[None], total[1][None])]
    psum x1 -> x0, waiting for transfers between devices: 94.9 us -> none  [on_device(): lax.psum(local[1].astype(jnp.bfloat16), 'dp').astype(jnp.float32)]
    convert_element_type x142 -> x2, other arithmetic: 77.3 us -> 1.14 us  [the longest x1 1.03 us: on_device(): own = jnp.stack([(gf * wa).astype(BF16), w_b[0]])]
  transfers between devices with their start and end apart: 117 -> 0, of which waited for: 41 -> 0; matrix products, arithmetic and copies ran while one was open for 21% -> 0% of each run, Pallas kernels for 0% -> 0%
where the time goes in v1:
time: 162 us; the launch traced here: 161 us
  Pallas kernels  151 us (93%)
  other arithmetic  6.15 us (4%)
  local copies, waits for them, and re-layouts  3.41 us (2%)
    pallas_call x1, Pallas kernels, gather(): pl.pallas_call(gather_kernel, out_shape=jax.ShapeDtypeStruct((2, S) + own...  64.9 us
    pallas_call x1, Pallas kernels, reduce(): pl.pallas_call(reduce_kernel, out_shape=jax.ShapeDtypeStruct((2, n, H, co...  37.2 us
    pallas_call x1, Pallas kernels, chain(): pl.pallas_call(chain_kernel, out_shape=(jax.ShapeDtypeStruct((S, 16, LANE...  21.7 us
    pallas_call x1, Pallas kernels, swap(): pl.pallas_call(swap_kernel, out_shape=(jax.ShapeDtypeStruct(msg.shape, ms...  17 us
    pallas_call x1, Pallas kernels, final(): pl.pallas_call(final_kernel, grid=(n,), out_shape=jax.ShapeDtypeStruct((n...  10.1 us

profile of v1, /device:TPU:1, one launch (start us, length us, event | category | flops | bytes accessed | tf_op | source)
XLA Modules:
  0.0 161.2 jit_solution(1082501239236664302)
XLA Ops:
  0.6 0.0 copy-start.2
  0.7 0.8 mul.34
  1.4 1.1 dynamic-slice_select_fusion
  2.5 0.7 pad_maximum_fusion.1.rows_ref
  3.2 1.0 fusion.2
  4.2 0.0 copy-done.2
  4.2 0.9 pad_maximum_fusion.own_ref
  5.1 64.9 %shard_map.94 = bf16[2,16,32,5120]{3,2,1,0:T(8,128)(2,1)} custom-call(bf16[2,32,5120]{2,1,0:T(8,128)(2,1)} %pad_maximum_fusion.own_ref), custom_call_target="tpu_custom_call" | custom-call | tf_op jit(solution)/shard_map/pallas_call | solution.py:379
  70.1 21.7 %shard_map.95 = (bf16[16,16,512]{2,1,0:T(8,128)(2,1)}, f32[16,8,128]{2,1,0:T(8,128)}) custom-call(bf16[16,5120]{1,0:T(8,128)(2,1)} %pad_maximum_fusion.1.rows_ref, bf16[1024,5120]{1,0:T(8,128)(2,1)} %bitcast.25), custom_call_target="tpu_custom_call" | custom-call | tf_op jit(solution)/shard_map/pallas_call | solution.py:118
  91.8 17.0 %shard_map.96 = (bf16[16,16,512]{2,1,0:T(8,128)(2,1)}, f32[16,8,128]{2,1,0:T(8,128)}) custom-call(bf16[16,16,512]{2,1,0:T(8,128)(2,1)} %get-tuple-element.7.msg_ref, f32[16,8,128]{2,1,0:T(8,128)} %get-tuple-element.8.sc_ref), custom_call_target="tpu_custom_call" | custom-call | tf_op jit(solution)/shard_map/pallas_call | solution.py:406
  108.8 10.1 %shard_map.97.g_ref = bf16[8,64,640]{2,1,0:T(8,128)(2,1)} custom-call(bf16[16,16,512]{2,1,0:T(8,128)(2,1)} %get-tuple-element.9.msg_ref, f32[16,8,128]{2,1,0:T(8,128)} %get-tuple-element.10.sc_ref, bf16[64,5120]{1,0:T(8,128)(2,1)} %bitcast.36, bf16[64,5120]{1,0:T(8,128)(2,1)} %bitcast.34, bf16[64,5120]{1,0:T(8,128)(2,1)} %bitcast.32, ...), custom_call_target="tpu_custom_call" | custom-call | tf_op jit(solution)/shard_map/pallas_call | solution.py:157
  118.9 0.0 copy-start
  118.9 1.1 copy-done
  120.0 37.2 %shard_map.98 = bf16[2,16,16,640]{3,2,1,0:T(8,128)(2,1)S(1)} custom-call(bf16[8,64,640]{2,1,0:T(8,128)(2,1)S(1)} %copy-done), custom_call_target="tpu_custom_call" | custom-call | tf_op jit(solution)/shard_map/pallas_call | solution.py:476
  157.2 0.1 convert_bitcast_fusion
  157.3 0.1 fusion.3
  157.4 0.2 copy.12
  157.6 0.9 slice.16
  158.5 0.0 copy-start.1
  158.5 0.2 copy.10
  158.7 0.1 copy.13
  158.9 0.6 copy-done.1
  159.5 0.7 fusion.1
  160.2 0.1 slice.14
  160.3 0.9 broadcast_multiply_fusion
Async XLA Ops:
  0.6 3.6 %copy-start.2 = (bf16[1,32,5120]{2,1,0:T(8,128)(2,1)S(1)}, bf16[1,32,5120]{2,1,0:T(8,128)(2,1)}, u32[]{:S(2)}) copy-start(bf16[1,32,5120]{2,1,0:T(8,128)(2,1)} %param.13) | copy-start | bytes 983044
  118.9 1.1 copy-start
  158.5 1.0 copy-start.1

commit v2 on v0

v2 whole, which is shorter than its diff:
```python
import jax
import jax.numpy as jnp
from jax import lax
from jax.experimental import pallas as pl
from jax.experimental.pallas import tpu as pltpu
from jax.sharding import PartitionSpec as P

F32, BF16 = jnp.float32, jnp.bfloat16
S, R, H = 16, 32, 16
ALL = S * R
ROWS = 128
MESH = pl.DeviceIdType.MESH
NT = (((1,), (1,)), ((), ()))
NN = (((1,), (0,)), ((), ()))

FIRST_A = (
    (0, "xl", 1), (0, "y1", 0, 0), (0, "xr", 0), (0, "xr", 1), (0, "y1", 0, 1), (0, "xl", 0),
)
ORDER_A = (
    (0, "y1", 0, 0), (0, "xl", 1), (0, "xr", 0), (0, "xl", 0), (0, "y1", 0, 1), (0, "x2r"),
    (0, "y1", 2, 1), (0, "y1", 1, 0), (0, "xr", 1), (0, "y1", 2, 0), (0, "y2", 0, 1), (0, "y2", 2, 1),
    (0, "y2", 0, 0), (0, "x2l"), (0, "y2", 1, 0), (0, "y1", 3, 0), (0, "y1", 1, 1), (0, "y3", 0),
    (0, "y2", 2, 0), (0, "y1", 3, 1), (0, "y2", 3, 0), (0, "y3", 1), (0, "y3", 2), (0, "y4", 0),
    (0, "y3", 3), (0, "y4", 1), (0, "y4", 3), (0, "y2", 1, 1), (0, "y4", 2), (0, "y2", 3, 1),
)
FIRST_B = (
    (1, "xr", 0, 1), (1, "xl", 0, 0), (1, "y1", 0), (1, "xl", 0, 1), (1, "y1", 1), (1, "xr", 0, 0),
)
ORDER_B = (
    (1, "y1", 0), (1, "y1", 1), (1, "xl", 0, 1), (1, "y2", 0), (1, "xr", 0, 0), (1, "xr", 1, 1),
    (1, "y2", 1), (1, "xr", 1, 0), (1, "xr", 0, 1), (1, "xl", 1, 1), (1, "y3"), (1, "xl", 2, 0),
    (1, "xl", 2, 1), (1, "xr", 2, 0), (1, "x2r", 0), (1, "y4"), (1, "xl", 3, 1), (1, "xr", 2, 1),
    (1, "x2l", 2), (1, "xl", 0, 0), (1, "x2r", 1), (1, "xl", 3, 0), (1, "x2r", 2), (1, "xl", 1, 0),
    (1, "xr", 3, 0), (1, "xr", 3, 1), (1, "x2l", 0), (1, "x2r", 3), (1, "x2l", 1), (1, "x2l", 3),
)


def dot(a, b, dims=NN):
    return lax.dot_general(a, b, dims, preferred_element_type=F32)


def gelu_pair(h):
    k = 0.7978845608028654
    t = jnp.tanh(k * (h + 0.044715 * h * h * h))
    up = 0.5 * (1.0 + t)
    return h * up, up + 0.5 * h * (1.0 - t * t) * (k * (1.0 + 3 * 0.044715 * h * h))


def halves(m):
    hi = m.astype(BF16)
    return hi, (m - hi.astype(F32)).astype(BF16)


class Place:
    def __init__(self):
        self.me, self.dp = lax.axis_index("section"), lax.axis_index("dp")
        self.deep = lax.axis_size("dp") // 4
        self.p, self.x = self.me // 4, lax.rem(self.me, 4)
        self.core = lax.rem(self.dp, 2)
        self.z = lax.rem(self.dp // 2, self.deep)
        self.y_lo = self.dp // (2 * self.deep)
        self.sgn = 2 * self.y_lo - 1
        other = self.dp + (1 - 2 * self.y_lo) * (2 * self.deep)
        self.right, self.left = (self.p * 4 + self.col(1), self.dp), (self.p * 4 + self.col(-1), self.dp)
        self.cross, self.pair = (self.row(self.sgn) * 4 + self.x, other), (self.me, other)
        self.sib = (self.me, self.dp + 1 - 2 * self.core)

    def row(self, d):
        return lax.rem(self.p + d + 4, 4)

    def col(self, d):
        return lax.rem(self.x + d + 4, 4)

    def spot(self, d, e):
        y = self.y_lo if e == 0 else 1 - self.y_lo
        z = lax.rem(self.z + d + self.deep, self.deep)
        return y, z, (self.me, (y * self.deep + z) * 2 + self.core)


def greet(partners):
    barrier = pltpu.get_barrier_semaphore()
    for partner in partners:
        pl.semaphore_signal(barrier, inc=1, device_id=partner, device_id_type=MESH)
    pl.semaphore_wait(barrier, len(partners))


def remote(src, dst, send, recv, to):
    return pltpu.make_async_remote_copy(src_ref=src, dst_ref=dst, send_sem=send, recv_sem=recv, device_id=to, device_id_type=MESH)


def route(at, name):
    me, p, x, y = at.me, at.p, at.x, at.y_lo
    hy = lambda h: y if h == 0 else 1 - y
    hn = lambda h: 1 - y if h == 0 else y
    near, away, far = at.row(at.sgn), at.row(-at.sgn), at.row(2)
    lft, rgt, opp = at.col(-1), at.col(1), at.col(2)
    kind, what, rest = name[0], name[1], name[2:]
    if kind == 0:
        if what in ("xr", "xl"):
            h = hy(rest[0])
            return (me, h), at.right if what == "xr" else at.left, (p * 4 + (lft if what == "xr" else rgt), h)
        if what == "x2r":
            return (p * 4 + lft, hy(0)), at.right, (p * 4 + opp, hy(0))
        if what == "x2l":
            return (p * 4 + rgt, hy(1)), at.left, (p * 4 + opp, hy(1))
        t = (x, lft, rgt, opp)[rest[0]]
        base, rest = p * 4 + t, rest[1:]
    else:
        if what in ("xr", "xl", "x2r", "x2l"):
            r = (p, near, away, far)[rest[0]]
            if what in ("xr", "xl"):
                h = hn(rest[1]) if rest[0] == 1 else hy(rest[1])
                return (r * 4 + x, h), at.right if what == "xr" else at.left, (r * 4 + (lft if what == "xr" else rgt), h)
            k = 0 if what == "x2r" else 1
            h = hn(k) if rest[0] == 1 else hy(k)
            return (r * 4 + (lft if k == 0 else rgt), h), at.right if k == 0 else at.left, (r * 4 + opp, h)
        t, base = x, me
    if what == "y1":
        return (base, hy(rest[0])), at.cross, (near * 4 + t, hn(rest[0]))
    if what == "y2":
        return (near * 4 + t, hn(rest[0])), at.pair, (away * 4 + t, hy(rest[0]))
    if what == "y3":
        return (away * 4 + t, y), at.cross, (far * 4 + t, 1 - y)
    return (far * 4 + t, 1 - y), at.pair, (far * 4 + t, y)


def needs(name):
    kind, what, rest = name[0], name[1], name[2:]
    if kind == 0:
        if what in ("xr", "xl"):
            return None
        if what == "x2r":
            return (0, "xr", 0)
        if what == "x2l":
            return (0, "xl", 1)
        t = rest[0]
        if what == "y1":
            return (None, (0, "xr", rest[1]), (0, "xl", rest[1]), (0, "x2r") if rest[1] == 0 else (0, "x2l"))[t]
        return {"y2": (0, "y1", t) + rest[1:], "y3": (0, "y2", t, 0), "y4": (0, "y3", t)}[what]
    if what == "y1":
        return None
    if what in ("y2", "y3", "y4"):
        return {"y2": (1, "y1") + rest, "y3": (1, "y2", 0), "y4": (1, "y3")}[what]
    if what in ("xr", "xl"):
        return (None, (1, "y1", rest[1]), (1, "y2", rest[1]), (1, "y4") if rest[1] == 0 else (1, "y3"))[rest[0]]
    return (1, "xr", rest[0], 0) if what == "x2r" else (1, "xl", rest[0], 1)


def spread(at, w, send, recv, prepare):
    def view(kind, unit):
        return w.at[kind, unit[0], pl.ds(pl.multiple_of(unit[1] * H, H), H)]

    def run(kind, first, order):
        slot = {name: i for i, name in enumerate(order)}
        sent = []

        def push(name):
            unit, to, _ = route(at, name)
            c = remote(view(kind, unit), view(kind, unit), send.at[slot[name]], recv.at[slot[name]], to)
            c.start()
            sent.append(c)

        for name in first:
            push(name)
        prepare()
        for i, name in enumerate(order):
            unit, to = route(at, name)[2], route(at, name)[1]
            got = view(kind, unit)
            remote(got, got, send.at[i], recv.at[i], to).wait_recv()
            for later in order:
                if needs(later) == name:
                    push(later)
            c = remote(got, got, send.at[32 + i], recv.at[32 + i], at.sib)
            c.start()
            sent.append(c)
        for c in sent:
            c.wait_send()

    def take(kind, order):
        for i, name in enumerate(order):
            got = view(kind, route(at, name)[2])
            remote(got, got, send.at[32 + i], recv.at[32 + i], at.sib).wait_recv()

    pl.when(at.core == 0)(lambda: run(0, FIRST_A, ORDER_A))
    pl.when(at.core == 1)(lambda: run(1, FIRST_B, ORDER_B))
    pl.when(at.core == 1)(lambda: take(0, ORDER_A))
    pl.when(at.core == 0)(lambda: take(1, ORDER_B))


def grams(w, rows, raw, gg, mm):
    width = rows.shape[1]

    def block(i, _):
        lhs = w[i // 2, pl.ds(lax.rem(i, 2) * 8, 8)].reshape(256, width)
        for b in range(2):
            raw[i, :, b * 256:(b + 1) * 256] = dot(lhs, w[1, b * 8:(b + 1) * 8].reshape(256, width), NT)
        raw[i, :, 512:768] = dot(lhs, rows[...], NT)
        raw[i, :, 768:896] = dot(lhs, jnp.ones((ROWS, width), BF16), NT)
        return 0

    lax.fori_loop(0, 4, block, 0)
    for i in range(4):
        for g in range(4):
            hi, lo = halves(raw[i, :, g * 128:(g + 1) * 128])
            gg[g, i * 256:(i + 1) * 256, 0:128] = hi
            gg[g, i * 256:(i + 1) * 256, 128:256] = lo
    for j in range(4):
        for s in range(j + 1):
            hi, lo = halves(raw[j // 2, (j % 2) * 128:(j % 2 + 1) * 128, s * 128:(s + 1) * 128].T)
            mm[j, s * 128:(s + 1) * 128, 0:128] = hi
            mm[j, s * 128:(s + 1) * 128, 128:256] = lo


def chain(width, stat, raw, gg, mm, u, v, c, acts, ds, fs, sc):
    for i in range(2):
        half = slice(i * 256, (i + 1) * 256)
        u[half] = raw[i, :, 640:768]
        v[half] = raw[2 + i, :, 640:768]
        c[half] = raw[2 + i, :, 512:640]

    def sums(kind, s):
        return raw[kind * 2 + s // 8, (s % 8) * R:(s % 8 + 1) * R, 768:896]

    def spot(a, s):
        o = s % 4
        parts = [jnp.zeros((o * R, ROWS), BF16)] * (o > 0) + [a] + [jnp.zeros(((3 - o) * R, ROWS), BF16)] * (o < 3)
        padded = jnp.concatenate(parts, axis=0) if len(parts) > 1 else a
        return jnp.concatenate([padded, padded], axis=0)

    total = lambda t: jnp.sum(t, axis=0, keepdims=True)
    mu, q = stat[0:1], stat[1:2]
    hid, slope, rstds, mus, kept, held = [], [], [], [], [], []
    for s in range(S):
        sl = slice(s * R, (s + 1) * R)
        rstd = lax.rsqrt(q * (1.0 / width) + 1e-5)
        h = rstd * (u[sl] - mu * sums(0, s))
        a, g = gelu_pair(h)
        a16 = a.astype(BF16)
        af = a16.astype(F32)
        acts[s] = a16
        old = v[sl]
        hid.append(h)
        slope.append(g)
        rstds.append(rstd)
        mus.append(mu)
        kept.append(old)
        held.append(af)
        if s < S - 1:
            rhs = spot(a16, s)
            wbs = sums(1, s)
            u[(s + 1) * R:] += dot(gg[s // 4, (s + 1) * R:ALL], rhs)
            new_v = v[s * R:] + dot(gg[s // 4, ALL + s * R:], rhs)
            v[s * R:] = new_v
            tot = total(af * wbs)
            q = q + total(af * (old + new_v[0:R] - (2.0 * mu) * wbs)) - tot * tot * (1.0 / width)
            q = jnp.maximum(q, 0.0)
            mu = mu + tot * (1.0 / width)
    cc, ee = jnp.zeros_like(mu), jnp.zeros_like(mu)
    blank = jnp.zeros((5, ROWS), F32)
    ds[S - 1] = jnp.zeros((R, ROWS), BF16)
    for j in range(S - 1, -1, -1):
        sl = slice(j * R, (j + 1) * R)
        sc[j] = jnp.concatenate([mus[j], cc, ee, blank], axis=0)
        da = c[sl] - cc * kept[j] - ee * sums(1, j)
        f16 = (rstds[j] * (da * slope[j])).astype(BF16)
        fs[j] = f16
        f = f16.astype(F32)
        a_j = total(f * sums(0, j)) * (1.0 / width)
        c_j = rstds[j] * total(f * hid[j]) * (1.0 / width)
        cc = cc + c_j
        ee = ee + a_j - c_j * mus[j]
        if j > 0:
            d16 = (held[j - 1] * cc).astype(BF16)
            ds[j - 1] = d16
            c[0:j * R] += dot(mm[j // 4, 0:j * R], spot(f16, j)) - dot(gg[(j - 1) // 4, ALL:ALL + j * R], spot(d16, j - 1))


def kernel(xd, xu, cd, cu, gain, wa, wb, gg_out, ga_out, gb_out,
           w, rows, stat, raw, gg, mm, u, v, c, acts, ds, fs, sc, half, near, part, pieces, total, tot,
           send, recv, rs_send, rs_recv, a2a_send, a2a_recv, ag_send, ag_recv, sh_send, sh_recv):
    at = Place()
    me, core, deep = at.me, at.core, at.deep
    width = rows.shape[1]
    step = width // deep
    far_first = sorted(range(deep), key=lambda d: (-min(d, deep - d), d))
    spots = [(k, e) for k in range(deep) for e in range(2) if (far_first[k], e) != (0, 0)]
    w[0, me] = (gain[...].astype(F32) * wa[...].astype(F32)).astype(BF16)
    w[1, me] = wb[...]
    greet([at.right, at.left, at.cross, at.sib] + [at.spot(far_first[k], e)[2] for k, e in spots])

    def prepare():
        for i, ref in enumerate((cd, cu, xd, xu)):
            for b in range(4):
                val = jnp.concatenate([ref[2 * b].astype(F32), ref[2 * b + 1].astype(F32)], axis=0)
                rows[i * 64 + b * 16:i * 64 + (b + 1) * 16] = val.astype(BF16)
        mus, qs = [], []
        for ref in (xd, xu):
            for b in range(8):
                val = ref[b].astype(F32)
                mean = jnp.sum(val, axis=1, keepdims=True) * (1.0 / width)
                val = val - mean
                mus.append(mean)
                qs.append(jnp.sum(val * val, axis=1, keepdims=True))
        wide = lambda t: jnp.broadcast_to(jnp.concatenate(t, axis=0), (ROWS, ROWS)).T[0:1]
        stat[0:1] = wide(mus)
        stat[1:2] = wide(qs)

    spread(at, w, send, recv, prepare)
    grams(w, rows, raw, gg, mm)
    chain(width, stat, raw, gg, mm, u, v, c, acts, ds, fs, sc)

    at_row = lax.broadcasted_iota(jnp.int32, (ALL, ROWS), 0)
    flat = lambda ref: ref[...].reshape(ALL, ROWS).astype(F32)
    turn = lambda t: t.T.astype(BF16)
    zx = turn(jnp.where(at_row < me * R, flat(acts), 0.0))
    zd = turn(jnp.where(at_row >= me * R, flat(ds), 0.0))
    fd = turn(jnp.where(at_row >= (me + 1) * R, flat(fs), 0.0))
    zxd = jnp.concatenate([zx, zd], axis=0)
    own = jnp.concatenate([sc[me], jnp.zeros((ROWS - 8, ROWS), F32)], axis=0).T
    mu, cc, ee = own[:, 0:1], own[:, 1:2], own[:, 2:3]
    act, f = acts[me], fs[me]

    def block(k):
        z = at.spot(far_first[k], 0)[1]
        cols = pl.ds(pl.multiple_of(z * step, step), step)
        from_b = dot(zxd, w[1, :, :, cols].reshape(ALL, step))
        x = rows[ROWS:, cols].astype(F32) + from_b[0:ROWS]
        dy = rows[0:ROWS, cols].astype(F32) + dot(fd, w[0, :, :, cols].reshape(ALL, step)) - from_b[ROWS:] - cc * x - ee
        half[k, 0:R] = dot(f, (x - mu).astype(BF16)).astype(BF16)
        half[k, R:] = dot(act, dy.astype(BF16)).astype(BF16)
        out = remote(half.at[k, pl.ds(pl.multiple_of((1 - core) * R, R), R)], near.at[k], rs_send.at[k], rs_recv.at[k], at.sib)
        out.start()
        return out

    def piece(k, e):
        y = at.y_lo if e == 0 else 1 - at.y_lo
        return part.at[k, pl.ds(pl.multiple_of(y * H, H), H)]

    out, moved = [], []
    for k in range(deep + 1):
        if k < deep:
            out.append(block(k))
        if k > 0:
            b = k - 1
            out[b].wait_recv()
            part[b] = (near[b].astype(F32) + half[b, pl.ds(pl.multiple_of(core * R, R), R)].astype(F32)).astype(BF16)
            for e in range(2):
                if (b, e) in spots:
                    n = 2 * b + e
                    moved.append(remote(piece(b, e), pieces.at[n], a2a_send.at[n], a2a_recv.at[n], at.spot(far_first[b], e)[2]))
                    moved[-1].start()
    acc = piece(far_first.index(0), 0)[...].astype(F32)
    for copy, (k, e) in zip(moved, spots):
        copy.wait_recv()
        acc = acc + pieces[2 * k + e].astype(F32)
    total[...] = acc.astype(BF16)

    def landing(kind, y, z):
        return tot.at[kind, pl.ds(pl.multiple_of(y * H, H), H), pl.ds(pl.multiple_of(z * step, step), step)]

    mine = landing(core, at.y_lo, at.z)
    for k, e in spots:
        n = 2 * k + e
        moved.append(remote(total, mine, ag_send.at[n], ag_recv.at[n], at.spot(far_first[k], e)[2]))
        moved[-1].start()
    mine[...] = total[...]
    moved.append(remote(mine, mine, sh_send.at[0], sh_recv.at[0], at.sib))
    moved[-1].start()
    came = [(at.y_lo, at.z)]
    for i, (k, e) in enumerate(spots):
        n = 2 * k + e
        y, z, to = at.spot(-far_first[k], e)
        got = landing(core, y, z)
        came.append((y, z))
        remote(got, got, ag_send.at[n], ag_recv.at[n], to).wait_recv()
        moved.append(remote(got, got, sh_send.at[1 + i], sh_recv.at[1 + i], at.sib))
        moved[-1].start()
    for i, (y, z) in enumerate(came):
        got = landing(1 - core, y, z)
        remote(got, got, sh_send.at[i], sh_recv.at[i], at.sib).wait_recv()
    for i in range(deep):
        cols = slice(i * step, (i + 1) * step)
        h = tot[0, :, cols].astype(F32)
        ga_out[:, cols] = gain[:, cols].astype(F32) * h
        gg_out[:, cols] = jnp.sum(wa[:, cols].astype(F32) * h, axis=0, keepdims=True)
        gb_out[:, cols] = tot[1, :, cols].astype(F32)
    for copy in out + moved:
        copy.wait_send()


def on_device(x_down, x_up, cot_down, cot_up, gain, w_a, w_b):
    width = x_down.shape[-1]
    deep = lax.axis_size("dp") // 4
    step = width // deep
    vmem = pl.BlockSpec(memory_space=pltpu.VMEM)
    sems = lambda n: [pltpu.SemaphoreType.DMA((n,)), pltpu.SemaphoreType.DMA((n,))]
    gg, ga, gb = pl.pallas_call(
        kernel,
        out_shape=(
            jax.ShapeDtypeStruct((1, width), F32),
            jax.ShapeDtypeStruct((R, width), F32),
            jax.ShapeDtypeStruct((R, width), F32),
        ),
        in_specs=[vmem] * 7,
        out_specs=(vmem,) * 3,
        scratch_shapes=[
            pltpu.VMEM((2, S, R, width), BF16),
            pltpu.VMEM((2 * ROWS, width), BF16),
            pltpu.VMEM((8, ROWS), F32),
            pltpu.VMEM((4, 256, 896), F32),
            pltpu.VMEM((4, 2 * ALL, 256), BF16),
            pltpu.VMEM((4, ALL, 256), BF16),
            pltpu.VMEM((ALL, ROWS), F32),
            pltpu.VMEM((ALL, ROWS), F32),
            pltpu.VMEM((ALL, ROWS), F32),
            pltpu.VMEM((S, R, ROWS), BF16),
            pltpu.VMEM((S, R, ROWS), BF16),
            pltpu.VMEM((S, R, ROWS), BF16),
            pltpu.VMEM((S, 8, ROWS), F32),
            pltpu.VMEM((deep, 2 * R, step), BF16),
            pltpu.VMEM((deep, R, step), BF16),
            pltpu.VMEM((deep, R, step), BF16),
            pltpu.VMEM((2 * deep, H, step), BF16),
            pltpu.VMEM((H, step), BF16),
            pltpu.VMEM((2, R, width), BF16),
        ]
        + sems(64) + sems(deep) + sems(2 * deep) + sems(2 * deep) + sems(2 * deep),
        compiler_params=pltpu.CompilerParams(collective_id=0, has_side_effects=True, vmem_limit_bytes=56 * 2**20),
    )(x_down[0], x_up[0], cot_down[0], cot_up[0], gain, w_a[0], w_b[0])
    return gg, ga[None], gb[None]


def solution(mesh):
    data, held = P("dp", None, None, None), P("section", None, None)
    return jax.shard_map(
        on_device,
        mesh=mesh,
        in_specs=(data, data, data, data, P("section", None), held, held),
        out_specs=(P("section", None), held, held),
        check_vma=False,
    )
```

time: 1670 us -> 104 us (0.06); the launches traced: 1640 us -> 103 us
  starting transfers between devices: 520 us -> 0 us
  other arithmetic: 316 us -> 0 us
  matrix products: 272 us -> 0 us
  waiting for transfers between devices: 263 us -> 0 us
  blocking collectives: 151 us -> 0 us
  Pallas kernels: 0 us -> 98.6 us
  local copies, waits for them, and re-layouts: 100 us -> 4.21 us
    ppermute x116 -> x0, starting transfers between devices: 520 us -> none  [the longest x92 364 us: passed_along(): return lax.ppermute(shard, axis, pairs)]
    dot_general x276 -> x0, matrix products: 272 us -> none  [the longest x46 80.8 us: section_backward(): lax.dot_general(normalized_output, w_a, (((1,), (1,)), ((), ())), preferr...]
    ppermute x116 -> x0, waiting for transfers between devices: 169 us -> none  [the longest x92 94.8 us: passed_along(): return lax.ppermute(shard, axis, pairs)]
    psum x1 -> x0, blocking collectives: 151 us -> none  [on_device(): lax.psum(local[0].astype(jnp.bfloat16), 'dp').astype(jnp.float32)]
    reduce_sum x184 -> x0, other arithmetic: 117 us -> none  [the longest x46 51.3 us: section_backward(): jnp.mean(centered_input * centered_input, axis=-1, keepdims=True) + 1e-05]
    pallas_call x0 -> x1, Pallas kernels: none -> 98.6 us  [on_device(): pl.pallas_call(kernel, out_shape=(jax.ShapeDtypeStruct((1, width), F32),...]
    psum x1 -> x0, waiting for transfers between devices: 94.9 us -> none  [on_device(): lax.psum(local[1].astype(jnp.bfloat16), 'dp').astype(jnp.float32)]
    convert_element_type x142 -> x0, other arithmetic: 77.3 us -> none  [the longest x46 75.7 us: section_backward(): (grad_y.astype(jnp.float32) + inverse_deviation * inner_product).astype(j...]
  transfers between devices with their start and end apart: 117 -> 0, of which waited for: 41 -> 0; matrix products, arithmetic and copies ran while one was open for 21% -> 0% of each run, Pallas kernels for 0% -> 0%
where the time goes in v2:
time: 104 us; the launch traced here: 103 us
  Pallas kernels  98.6 us (95%)
  local copies, waits for them, and re-layouts  4.21 us (4%)
    pallas_call x1, Pallas kernels, on_device(): pl.pallas_call(kernel, out_shape=(jax.ShapeDtypeStruct((1, width), F32),...  98.6 us
    unnamed x5, local copies, waits for them, and re-layouts  4.21 us

profile of v2, /device:TPU:1, one launch (start us, length us, event | category | flops | bytes accessed | tf_op | source)
XLA Modules:
  0.0 103.4 jit_solution(16423967865471398052)
XLA Ops:
  0.6 98.6 %shard_map.94 = (f32[1,5120]{1,0:T(1,128)}, f32[32,5120]{1,0:T(8,128)}, f32[32,5120]{1,0:T(8,128)}) custom-call(bf16[8,8,5120]{2,1,0:T(8,128)(2,1)} %bitcast.10, bf16[8,8,5120]{2,1,0:T(8,128)(2,1)} %bitcast.11, bf16[8,8,5120]{2,1,0:T(8,128)(2,1)} %bitcast.12, bf16[8,8,5120]{2,1,0:T(8,128)(2,1)} %bitcast.13, bf16[1,5120]{1,0:T(2,128)(2,1)} %gain.1, ...), custom_call_target="tpu_custom_call" | custom-call | tf_op jit(solution)/shard_map/pallas_call | solution.py:397
  99.2 1.3 %copy.13 = f32[1,5120]{1,0:T(1,128)} copy(f32[1,5120]{1,0:T(1,128)} %get-tuple-element.12) | data formatting | bytes 40960
  100.6 0.0 copy-start
  100.6 2.0 %copy.14 = f32[1,32,5120]{2,1,0:T(8,128)} copy(f32[1,32,5120]{2,1,0:T(8,128)} %bitcast.9) | data formatting | bytes 1310720
  102.6 0.0 copy-done
  102.6 0.8 copy.15
Async XLA Ops:
  100.6 2.0 %copy-start = (f32[32,5120]{1,0:T(8,128)S(1)}, f32[32,5120]{1,0:T(8,128)}, u32[]{:S(2)}) copy-start(f32[32,5120]{1,0:T(8,128)} %get-tuple-element.8) | copy-start | bytes 1966084

commit v3 on v2

--- a/solution.py
+++ b/solution.py
@@ -14,24 +14,40 @@
 NN = (((1,), (0,)), ((), ()))
 
 FIRST_A = (
-    (0, "xl", 1), (0, "y1", 0, 0), (0, "xr", 0), (0, "xr", 1), (0, "y1", 0, 1), (0, "xl", 0),
+    (0, "xl", 0), (0, "xr", 0), (0, "xr", 1), (0, "y1", 0, 0), (0, "y1", 0, 1), (0, "xl", 1),
 )
 ORDER_A = (
-    (0, "y1", 0, 0), (0, "xl", 1), (0, "xr", 0), (0, "xl", 0), (0, "y1", 0, 1), (0, "x2r"),
-    (0, "y1", 2, 1), (0, "y1", 1, 0), (0, "xr", 1), (0, "y1", 2, 0), (0, "y2", 0, 1), (0, "y2", 2, 1),
-    (0, "y2", 0, 0), (0, "x2l"), (0, "y2", 1, 0), (0, "y1", 3, 0), (0, "y1", 1, 1), (0, "y3", 0),
-    (0, "y2", 2, 0), (0, "y1", 3, 1), (0, "y2", 3, 0), (0, "y3", 1), (0, "y3", 2), (0, "y4", 0),
-    (0, "y3", 3), (0, "y4", 1), (0, "y4", 3), (0, "y2", 1, 1), (0, "y4", 2), (0, "y2", 3, 1),
+    (0, "xr", 0), (0, "y1", 0, 0), (0, "xl", 0), (0, "xr", 1), (0, "y1", 0, 1), (0, "xl", 1),
+    (0, "x2r", 0), (0, "y1", 1, 0), (0, "x2l", 0), (0, "y1", 2, 0), (0, "x2r", 1), (0, "y1", 1, 1),
+    (0, "x2l", 1), (0, "z", 3), (0, "z", 6), (0, "y2", 0, 0), (0, "z", 0), (0, "y1", 2, 1),
+    (0, "y2", 1, 0), (0, "y1", 3, 0), (0, "y2", 2, 0), (0, "y2", 0, 1), (0, "y2", 1, 1), (0, "y1", 3, 1),
+    (0, "y2", 2, 1), (0, "y3", 1, 0), (0, "y2", 3, 0), (0, "z", 1), (0, "z", 7), (0, "y3", 0, 0),
+    (0, "y3", 2, 0), (0, "y3", 1, 1), (0, "z", 12), (0, "y2", 3, 1), (0, "z", 4), (0, "y3", 3, 0),
+    (0, "y4", 1, 0), (0, "y4", 0, 0), (0, "y3", 0, 1), (0, "y4", 2, 0), (0, "z", 9), (0, "y3", 2, 1),
+    (0, "y4", 1, 1), (0, "y3", 3, 1), (0, "y4", 3, 0), (0, "z", 10), (0, "y4", 0, 1), (0, "z", 11),
+    (0, "y4", 2, 1), (0, "z", 8), (0, "z", 5), (0, "y4", 3, 1), (0, "z", 2), (0, "z", 13),
+    (0, "z", 14),
 )
 FIRST_B = (
-    (1, "xr", 0, 1), (1, "xl", 0, 0), (1, "y1", 0), (1, "xl", 0, 1), (1, "y1", 1), (1, "xr", 0, 0),
+    (1, "y1", 0), (1, "y1", 1), (1, "xr", 0, 0), (1, "xr", 0, 1), (1, "xl", 0, 0), (1, "xl", 0, 1),
 )
 ORDER_B = (
-    (1, "y1", 0), (1, "y1", 1), (1, "xl", 0, 1), (1, "y2", 0), (1, "xr", 0, 0), (1, "xr", 1, 1),
-    (1, "y2", 1), (1, "xr", 1, 0), (1, "xr", 0, 1), (1, "xl", 1, 1), (1, "y3"), (1, "xl", 2, 0),
-    (1, "xl", 2, 1), (1, "xr", 2, 0), (1, "x2r", 0), (1, "y4"), (1, "xl", 3, 1), (1, "xr", 2, 1),
-    (1, "x2l", 2), (1, "xl", 0, 0), (1, "x2r", 1), (1, "xl", 3, 0), (1, "x2r", 2), (1, "xl", 1, 0),
-    (1, "xr", 3, 0), (1, "xr", 3, 1), (1, "x2l", 0), (1, "x2r", 3), (1, "x2l", 1), (1, "x2l", 3),
+    (1, "y1", 0), (1, "xr", 0, 0), (1, "y1", 1), (1, "xl", 0, 0), (1, "xl", 0, 1), (1, "y2", 0),
+    (1, "xr", 0, 1), (1, "xl", 1, 1), (1, "xl", 1, 0), (1, "y2", 1), (1, "xr", 1, 1), (1, "y3", 0),
+    (1, "xr", 1, 0), (1, "xr", 2, 0), (1, "x2l", 1, 1), (1, "z", 0), (1, "xl", 2, 0), (1, "x2l", 0, 0),
+    (1, "x2l", 0, 1), (1, "y3", 1), (1, "x2r", 0, 1), (1, "xr", 2, 1), (1, "z", 4), (1, "y4", 0),
+    (1, "x2r", 0, 0), (1, "x2r", 1, 0), (1, "x2l", 2, 0), (1, "x2l", 1, 0), (1, "z", 3), (1, "y4", 1),
+    (1, "x2r", 2, 0), (1, "xr", 3, 0), (1, "xl", 3, 0), (1, "xl", 2, 1), (1, "x2r", 1, 1), (1, "z", 5),
+    (1, "xr", 3, 1), (1, "x2r", 3, 0), (1, "x2l", 3, 0), (1, "xl", 3, 1), (1, "x2l", 2, 1), (1, "z", 9),
+    (1, "z", 13), (1, "z", 10), (1, "z", 2), (1, "x2r", 3, 1), (1, "z", 6), (1, "z", 8),
+    (1, "z", 7), (1, "x2r", 2, 1), (1, "z", 12), (1, "z", 14), (1, "z", 11), (1, "x2l", 3, 1),
+    (1, "z", 1),
+)
+BROUGHT = (
+    [((0, "xr"),), ((0, "xl"),), ((0, "x2r"), (0, "x2l"))]
+    + [b for t in range(4) for b in (((0, "y1", t),), ((0, "y2", t),), ((0, "y3", t), (0, "y4", t)))],
+    [((1, "y1"),), ((1, "y2"),), ((1, "y3"), (1, "y4"))]
+    + [b for r in range(4) for b in (((1, "xr", r),), ((1, "xl", r),), ((1, "x2r", r), (1, "x2l", r)))],
 )
 
 
@@ -89,98 +105,137 @@
 
 
 def route(at, name):
-    me, p, x, y = at.me, at.p, at.x, at.y_lo
-    hy = lambda h: y if h == 0 else 1 - y
-    hn = lambda h: 1 - y if h == 0 else y
+    p, x, y = at.p, at.x, at.y_lo
     near, away, far = at.row(at.sgn), at.row(-at.sgn), at.row(2)
     lft, rgt, opp = at.col(-1), at.col(1), at.col(2)
-    kind, what, rest = name[0], name[1], name[2:]
-    if kind == 0:
-        if what in ("xr", "xl"):
-            h = hy(rest[0])
-            return (me, h), at.right if what == "xr" else at.left, (p * 4 + (lft if what == "xr" else rgt), h)
-        if what == "x2r":
-            return (p * 4 + lft, hy(0)), at.right, (p * 4 + opp, hy(0))
-        if what == "x2l":
-            return (p * 4 + rgt, hy(1)), at.left, (p * 4 + opp, hy(1))
-        t = (x, lft, rgt, opp)[rest[0]]
-        base, rest = p * 4 + t, rest[1:]
-    else:
-        if what in ("xr", "xl", "x2r", "x2l"):
-            r = (p, near, away, far)[rest[0]]
-            if what in ("xr", "xl"):
-                h = hn(rest[1]) if rest[0] == 1 else hy(rest[1])
-                return (r * 4 + x, h), at.right if what == "xr" else at.left, (r * 4 + (lft if what == "xr" else rgt), h)
-            k = 0 if what == "x2r" else 1
-            h = hn(k) if rest[0] == 1 else hy(k)
-            return (r * 4 + (lft if k == 0 else rgt), h), at.right if k == 0 else at.left, (r * 4 + opp, h)
-        t, base = x, me
-    if what == "y1":
-        return (base, hy(rest[0])), at.cross, (near * 4 + t, hn(rest[0]))
-    if what == "y2":
-        return (near * 4 + t, hn(rest[0])), at.pair, (away * 4 + t, hy(rest[0]))
-    if what == "y3":
-        return (away * 4 + t, y), at.cross, (far * 4 + t, 1 - y)
-    return (far * 4 + t, 1 - y), at.pair, (far * 4 + t, y)
+    kind, what = name[0], name[1]
+    if what[0] == "x":
+        r = (p, near, away, far)[name[2] if kind else 0] * 4
+        return {
+            "xr": ((r + x, None), at.right, (r + lft, None)),
+            "xl": ((r + x, None), at.left, (r + rgt, None)),
+            "x2r": ((r + lft, y), at.right, (r + opp, y)),
+            "x2l": ((r + rgt, 1 - y), at.left, (r + opp, 1 - y)),
+        }[what]
+    t = x if kind else (x, lft, rgt, opp)[name[2]]
+    return {
+        "y1": ((p * 4 + t, None), at.cross, (near * 4 + t, None)),
+        "y2": ((near * 4 + t, None), at.pair, (away * 4 + t, None)),
+        "y3": ((away * 4 + t, y), at.cross, (far * 4 + t, 1 - y)),
+        "y4": ((far * 4 + t, 1 - y), at.pair, (far * 4 + t, y)),
+    }[what]
 
 
 def needs(name):
-    kind, what, rest = name[0], name[1], name[2:]
-    if kind == 0:
-        if what in ("xr", "xl"):
-            return None
-        if what == "x2r":
-            return (0, "xr", 0)
-        if what == "x2l":
-            return (0, "xl", 1)
-        t = rest[0]
-        if what == "y1":
-            return (None, (0, "xr", rest[1]), (0, "xl", rest[1]), (0, "x2r") if rest[1] == 0 else (0, "x2l"))[t]
-        return {"y2": (0, "y1", t) + rest[1:], "y3": (0, "y2", t, 0), "y4": (0, "y3", t)}[what]
-    if what == "y1":
-        return None
+    kind, what, rest, q = name[0], name[1], name[2:-1], name[-1:]
+    if what == "z":
+        return [base + (0,) for base in BROUGHT[kind][name[2]]]
+    if what in ("x2r", "x2l"):
+        return [(kind, "xr" if what == "x2r" else "xl") + rest + q]
     if what in ("y2", "y3", "y4"):
-        return {"y2": (1, "y1") + rest, "y3": (1, "y2", 0), "y4": (1, "y3")}[what]
-    if what in ("xr", "xl"):
-        return (None, (1, "y1", rest[1]), (1, "y2", rest[1]), (1, "y4") if rest[1] == 0 else (1, "y3"))[rest[0]]
-    return (1, "xr", rest[0], 0) if what == "x2r" else (1, "xl", rest[0], 1)
-
-
-def spread(at, w, send, recv, prepare):
-    def view(kind, unit):
-        return w.at[kind, unit[0], pl.ds(pl.multiple_of(unit[1] * H, H), H)]
+        return [(kind, {"y2": "y1", "y3": "y2", "y4": "y3"}[what]) + rest + q]
+    if kind == 0 and what == "y1":
+        return [[], [(0, "xr") + q], [(0, "xl") + q], [(0, "x2r") + q, (0, "x2l") + q]][rest[0]]
+    if kind == 1 and what in ("xr", "xl"):
+        return [[], [(1, "y1") + q], [(1, "y2") + q], [(1, "y3") + q, (1, "y4") + q]][rest[0]]
+    return []
+
+
+def sum_tiles(w, kind, sec, first, last):
+    acc = w[kind, sec, :, first:first + 128].astype(F32)
+    for col in range(first + 128, last, 128):
+        acc = acc + w[kind, sec, :, col:col + 128].astype(F32)
+    return acc
+
+
+def spread(at, w, sums, send, recv, prepare):
+    width = w.shape[-1]
+    part = width // 128 * 3 // 10 * 128
+    parity = lax.rem(at.z, 2)
+    up, down = at.spot(1, 0)[2], at.spot(-1, 0)[2]
+
+    def view(kind, unit, q):
+        rows = pl.ds(0, R) if unit[1] is None else pl.ds(pl.multiple_of(unit[1] * H, H), H)
+        cols = pl.ds(2 * part, width - 2 * part) if q else pl.ds(pl.multiple_of(parity * part, 128), part)
+        return w.at[kind, unit[0], rows, cols]
+
+    def strip(kind, sec, side, which):
+        start = side * part + which * (part // 2)
+        return w.at[kind, sec, :, pl.ds(pl.multiple_of(start, 128), part // 2)]
+
+    def handed(kind, sec, q):
+        return w.at[kind, sec, :, pl.ds(2 * part, width - 2 * part) if q else pl.ds(0, 2 * part)]
+
+    def tally(kind, sec, q):
+        sums[kind, sec] += sum_tiles(w, kind, sec, 2 * part if q else 0, width if q else 2 * part)
+
+    def section(kind, i):
+        return route(at, BROUGHT[kind][i][0])[2][0]
+
+    def ends(kind, order):
+        found = []
+        for n, name in enumerate(order):
+            if name[1] == "z":
+                found.append((n, name[2], 0))
+            elif name[-1] == 1:
+                for i, bases in enumerate(BROUGHT[kind]):
+                    if name[:-1] in bases and all(order.index(base + (1,)) <= n for base in bases):
+                        found.append((n, i, 1))
+        return found
 
     def run(kind, first, order):
-        slot = {name: i for i, name in enumerate(order)}
-        sent = []
-
-        def push(name):
-            unit, to, _ = route(at, name)
-            c = remote(view(kind, unit), view(kind, unit), send.at[slot[name]], recv.at[slot[name]], to)
+        sent, seen = [], set()
+        over = {n: (i, q) for n, i, q in ends(kind, order)}
+
+        def start(src, dst, index, to):
+            c = remote(src, dst, send.at[index], recv.at[index], to)
             c.start()
             sent.append(c)
+
+        def push(name):
+            n = order.index(name)
+            if name[1] == "z":
+                for which, index, to in ((0, n, up), (1, 55 + name[2], down)):
+                    mine = strip(kind, section(kind, name[2]), parity, which)
+                    start(mine, mine, index, to)
+            else:
+                unit, to, _ = route(at, name)
+                start(view(kind, unit, name[-1]), view(kind, unit, name[-1]), n, to)
 
         for name in first:
             push(name)
         prepare()
-        for i, name in enumerate(order):
-            unit, to = route(at, name)[2], route(at, name)[1]
-            got = view(kind, unit)
-            remote(got, got, send.at[i], recv.at[i], to).wait_recv()
+        for n, name in enumerate(order):
+            if name[1] == "z":
+                for which, index, to in ((0, n, up), (1, 55 + name[2], down)):
+                    got = strip(kind, section(kind, name[2]), 1 - parity, which)
+                    remote(got, got, send.at[index], recv.at[index], to).wait_recv()
+            else:
+                got = view(kind, route(at, name)[2], name[-1])
+                remote(got, got, send.at[n], recv.at[n], at.right).wait_recv()
+            seen.add(name)
             for later in order:
-                if needs(later) == name:
+                if name in needs(later) and seen.issuperset(needs(later)):
                     push(later)
-            c = remote(got, got, send.at[32 + i], recv.at[32 + i], at.sib)
-            c.start()
-            sent.append(c)
+            if n in over:
+                i, q = over[n]
+                got = handed(kind, section(kind, i), q)
+                start(got, got, 70 + 15 * q + i, at.sib)
+                tally(kind, section(kind, i), q)
         for c in sent:
             c.wait_send()
 
     def take(kind, order):
-        for i, name in enumerate(order):
-            got = view(kind, route(at, name)[2])
-            remote(got, got, send.at[32 + i], recv.at[32 + i], at.sib).wait_recv()
-
+        for _, i, q in ends(kind, order):
+            sec = section(kind, i)
+            got = handed(kind, sec, q)
+            remote(got, got, send.at[70 + 15 * q + i], recv.at[70 + 15 * q + i], at.sib).wait_recv()
+            tally(kind, sec, q)
+
+    sums[...] = jnp.zeros_like(sums)
+    for kind in range(2):
+        for q in range(2):
+            tally(kind, at.me, q)
     pl.when(at.core == 0)(lambda: run(0, FIRST_A, ORDER_A))
     pl.when(at.core == 1)(lambda: run(1, FIRST_B, ORDER_B))
     pl.when(at.core == 1)(lambda: take(0, ORDER_A))
@@ -189,37 +244,47 @@
 
 def grams(w, rows, raw, gg, mm):
     width = rows.shape[1]
-
-    def block(i, _):
-        lhs = w[i // 2, pl.ds(lax.rem(i, 2) * 8, 8)].reshape(256, width)
-        for b in range(2):
-            raw[i, :, b * 256:(b + 1) * 256] = dot(lhs, w[1, b * 8:(b + 1) * 8].reshape(256, width), NT)
-        raw[i, :, 512:768] = dot(lhs, rows[...], NT)
-        raw[i, :, 768:896] = dot(lhs, jnp.ones((ROWS, width), BF16), NT)
+    tile = lambda b: w[1, b * 8:(b + 1) * 8].reshape(256, width)
+
+    def block(kind, _):
+        for i in range(2):
+            lhs = w[kind, i * 8:(i + 1) * 8].reshape(256, width)
+            for b in range(i + 1):
+                raw[2 * kind + i, :, b * 256:(b + 1) * 256] = dot(lhs, tile(b), NT)
+            raw[2 * kind + i, :, 512:768] = dot(lhs, rows[...], NT)
         return 0
 
-    lax.fori_loop(0, 4, block, 0)
+    lax.fori_loop(0, 2, block, 0)
+
+    def keep(ref, g, first, value):
+        hi, lo = halves(value)
+        ref[g, first:first + value.shape[0], 0:128] = hi
+        ref[g, first:first + value.shape[0], 128:256] = lo
+
     for i in range(4):
-        for g in range(4):
-            hi, lo = halves(raw[i, :, g * 128:(g + 1) * 128])
-            gg[g, i * 256:(i + 1) * 256, 0:128] = hi
-            gg[g, i * 256:(i + 1) * 256, 128:256] = lo
+        for g in range(2 * (i % 2) + 2):
+            keep(gg, g, i * 256, raw[i, :, g * 128:(g + 1) * 128])
+    for g in range(2):
+        for t in range(2):
+            keep(gg, 2 + g, ALL + t * 128, raw[3, g * 128:(g + 1) * 128, t * 128:(t + 1) * 128].T)
     for j in range(4):
         for s in range(j + 1):
-            hi, lo = halves(raw[j // 2, (j % 2) * 128:(j % 2 + 1) * 128, s * 128:(s + 1) * 128].T)
-            mm[j, s * 128:(s + 1) * 128, 0:128] = hi
-            mm[j, s * 128:(s + 1) * 128, 128:256] = lo
-
-
-def chain(width, stat, raw, gg, mm, u, v, c, acts, ds, fs, sc):
+            keep(mm, j, s * 128, raw[j // 2, (j % 2) * 128:(j % 2 + 1) * 128, s * 128:(s + 1) * 128].T)
+
+
+def chain(width, stat, row_sums, raw, gg, mm, u, v, c, acts, ds, fs, sc):
     for i in range(2):
         half = slice(i * 256, (i + 1) * 256)
         u[half] = raw[i, :, 640:768]
         v[half] = raw[2 + i, :, 640:768]
         c[half] = raw[2 + i, :, 512:640]
 
+    for kind in range(2):
+        for s in range(S):
+            row_sums[kind, s] = jnp.broadcast_to(jnp.sum(row_sums[kind, s], axis=1, keepdims=True), (R, ROWS))
+
     def sums(kind, s):
-        return raw[kind * 2 + s // 8, (s % 8) * R:(s % 8 + 1) * R, 768:896]
+        return row_sums[kind, s]
 
     def spot(a, s):
         o = s % 4
@@ -275,8 +340,8 @@
             c[0:j * R] += dot(mm[j // 4, 0:j * R], spot(f16, j)) - dot(gg[(j - 1) // 4, ALL:ALL + j * R], spot(d16, j - 1))
 
 
-def kernel(xd, xu, cd, cu, gain, wa, wb, gg_out, ga_out, gb_out,
-           w, rows, stat, raw, gg, mm, u, v, c, acts, ds, fs, sc, half, near, part, pieces, total, tot,
+def kernel(xd, xu, cd, cu, gain, wa, wb, tot,
+           w, rows, stat, row_sums, raw, gg, mm, u, v, c, acts, ds, fs, sc, half, near, part, pieces, total,
            send, recv, rs_send, rs_recv, a2a_send, a2a_recv, ag_send, ag_recv, sh_send, sh_recv):
     at = Place()
     me, core, deep = at.me, at.core, at.deep
@@ -305,9 +370,9 @@
         stat[0:1] = wide(mus)
         stat[1:2] = wide(qs)
 
-    spread(at, w, send, recv, prepare)
+    spread(at, w, row_sums, send, recv, prepare)
     grams(w, rows, raw, gg, mm)
-    chain(width, stat, raw, gg, mm, u, v, c, acts, ds, fs, sc)
+    chain(width, stat, row_sums, raw, gg, mm, u, v, c, acts, ds, fs, sc)
 
     at_row = lax.broadcasted_iota(jnp.int32, (ALL, ROWS), 0)
     flat = lambda ref: ref[...].reshape(ALL, ROWS).astype(F32)
@@ -378,12 +443,6 @@
     for i, (y, z) in enumerate(came):
         got = landing(1 - core, y, z)
         remote(got, got, sh_send.at[i], sh_recv.at[i], at.sib).wait_recv()
-    for i in range(deep):
-        cols = slice(i * step, (i + 1) * step)
-        h = tot[0, :, cols].astype(F32)
-        ga_out[:, cols] = gain[:, cols].astype(F32) * h
-        gg_out[:, cols] = jnp.sum(wa[:, cols].astype(F32) * h, axis=0, keepdims=True)
-        gb_out[:, cols] = tot[1, :, cols].astype(F32)
     for copy in out + moved:
         copy.wait_send()
 
@@ -394,20 +453,17 @@
     step = width // deep
     vmem = pl.BlockSpec(memory_space=pltpu.VMEM)
     sems = lambda n: [pltpu.SemaphoreType.DMA((n,)), pltpu.SemaphoreType.DMA((n,))]
-    gg, ga, gb = pl.pallas_call(
+    total = pl.pallas_call(
         kernel,
-        out_shape=(
-            jax.ShapeDtypeStruct((1, width), F32),
-            jax.ShapeDtypeStruct((R, width), F32),
-            jax.ShapeDtypeStruct((R, width), F32),
-        ),
+        out_shape=jax.ShapeDtypeStruct((2, R, width), BF16),
         in_specs=[vmem] * 7,
-        out_specs=(vmem,) * 3,
+        out_specs=vmem,
         scratch_shapes=[
             pltpu.VMEM((2, S, R, width), BF16),
             pltpu.VMEM((2 * ROWS, width), BF16),
             pltpu.VMEM((8, ROWS), F32),
-            pltpu.VMEM((4, 256, 896), F32),
+            pltpu.VMEM((2, S, R, ROWS), F32),
+            pltpu.VMEM((4, 256, 768), F32),
             pltpu.VMEM((4, 2 * ALL, 256), BF16),
             pltpu.VMEM((4, ALL, 256), BF16),
             pltpu.VMEM((ALL, ROWS), F32),
@@ -422,12 +478,12 @@
             pltpu.VMEM((deep, R, step), BF16),
             pltpu.VMEM((2 * deep, H, step), BF16),
             pltpu.VMEM((H, step), BF16),
-            pltpu.VMEM((2, R, width), BF16),
         ]
-        + sems(64) + sems(deep) + sems(2 * deep) + sems(2 * deep) + sems(2 * deep),
+        + sems(100) + sems(deep) + sems(2 * deep) + sems(2 * deep) + sems(2 * deep),
         compiler_params=pltpu.CompilerParams(collective_id=0, has_side_effects=True, vmem_limit_bytes=56 * 2**20),
     )(x_down[0], x_up[0], cot_down[0], cot_up[0], gain, w_a[0], w_b[0])
-    return gg, ga[None], gb[None]
+    h = total[0].astype(F32)
+    return jnp.sum(w_a[0].astype(F32) * h, axis=0)[None], (gain.astype(F32) * h)[None], total[1].astype(F32)[None]
 
 
 def solution(mesh):

time: 104 us -> 94.5 us (0.909)
  Pallas kernels: 98.6 us -> 89.4 us
  other arithmetic: 0 us -> 4.28 us
  local copies, waits for them, and re-layouts: 4.21 us -> 0.01 us
    pallas_call x1, Pallas kernels: 98.6 us -> 89.4 us  [on_device(): pl.pallas_call(kernel, out_shape=jax.ShapeDtypeStruct((2, R, width), BF16...]
    unnamed x5 -> x4, local copies, waits for them, and re-layouts: 4.21 us -> 0.01 us
    reduce_sum x0 -> x1, other arithmetic: none -> 1.76 us  [on_device(): jnp.sum(w_a[0].astype(F32) * h, axis=0)[None]]
    mul x0 -> x2, other arithmetic: none -> 1.64 us  [on_device(): gain.astype(F32) * h]
where the time goes in v3:
time: 94.5 us; the launch traced here: 94.3 us
  Pallas kernels  89.4 us (95%)
  other arithmetic  4.28 us (5%)
    pallas_call x1, Pallas kernels, on_device(): pl.pallas_call(kernel, out_shape=jax.ShapeDtypeStruct((2, R, width), BF16...  89.4 us

profile of v3, /device:TPU:1, one launch (start us, length us, event | category | flops | bytes accessed | tf_op | source)
XLA Modules:
  0.0 94.3 jit_solution(10658240614541633034)
XLA Ops:
  0.6 0.8 mul.21
  1.4 0.0 copy-start.1
  1.4 89.4 %shard_map.94 = bf16[2,32,5120]{2,1,0:T(8,128)(2,1)} custom-call(bf16[8,8,5120]{2,1,0:T(8,128)(2,1)} %bitcast.16, bf16[8,8,5120]{2,1,0:T(8,128)(2,1)} %bitcast.17, bf16[8,8,5120]{2,1,0:T(8,128)(2,1)} %bitcast.18, bf16[8,8,5120]{2,1,0:T(8,128)(2,1)} %bitcast.19, bf16[1,5120]{1,0:T(2,128)(2,1)} %gain.1, bf16[32,5120]{1,0:T(8,128)(2,1)} %bitcast.15, ...), custom_call_target="tpu_custom_call" | custom-call | tf_op jit(solution)/shard_map/pallas_call | solution.py:456
  90.8 0.0 copy-done.1
  90.8 0.0 copy-start
  90.8 1.8 %fusion.1 = f32[5120]{0:T(1024)} fusion(bf16[2,32,5120]{2,1,0:T(8,128)(2,1)} %shard_map.94, bf16[1,32,5120]{2,1,0:T(8,128)(2,1)S(1)} %copy-done.1), kind=kLoop, calls=%fused_computation.3 | loop fusion | flops 650240 | bytes 675840 | tf_op jit(solution)/shard_map/reduce_sum | solution.py:486
  92.6 0.0 copy-done
  92.6 0.9 convert_multiply_fusion
  93.5 0.9 slice_convert_fusion
Async XLA Ops:
  1.4 89.4 %copy-start.1 = (bf16[1,32,5120]{2,1,0:T(8,128)(2,1)S(1)}, bf16[1,32,5120]{2,1,0:T(8,128)(2,1)}, u32[]{:S(2)}) copy-start(bf16[1,32,5120]{2,1,0:T(8,128)(2,1)} %param.12) | copy-start | bytes 983044
  90.8 1.8 %copy-start = (bf16[2,32,5120]{2,1,0:T(8,128)(2,1)S(1)}, bf16[2,32,5120]{2,1,0:T(8,128)(2,1)}, u32[]{:S(2)}) copy-start(bf16[2,32,5120]{2,1,0:T(8,128)(2,1)} %shard_map.94) | copy-start | bytes 1966084

commit v4 on v3

--- a/solution.py
+++ b/solution.py
@@ -93,10 +93,11 @@
         return y, z, (self.me, (y * self.deep + z) * 2 + self.core)
 
 
-def greet(partners):
+def greet(partners, meanwhile):
     barrier = pltpu.get_barrier_semaphore()
     for partner in partners:
         pl.semaphore_signal(barrier, inc=1, device_id=partner, device_id_type=MESH)
+    meanwhile()
     pl.semaphore_wait(barrier, len(partners))
 
 
@@ -141,10 +142,10 @@
     return []
 
 
-def sum_tiles(w, kind, sec, first, last):
-    acc = w[kind, sec, :, first:first + 128].astype(F32)
+def sum_tiles(w, sec, first, last):
+    acc = w[1, sec, :, first:first + 128].astype(F32)
     for col in range(first + 128, last, 128):
-        acc = acc + w[kind, sec, :, col:col + 128].astype(F32)
+        acc = acc + w[1, sec, :, col:col + 128].astype(F32)
     return acc
 
 
@@ -166,8 +167,8 @@
     def handed(kind, sec, q):
         return w.at[kind, sec, :, pl.ds(2 * part, width - 2 * part) if q else pl.ds(0, 2 * part)]
 
-    def tally(kind, sec, q):
-        sums[kind, sec] += sum_tiles(w, kind, sec, 2 * part if q else 0, width if q else 2 * part)
+    def tally(sec, q):
+        sums[sec] += sum_tiles(w, sec, 2 * part if q else 0, width if q else 2 * part)
 
     def section(kind, i):
         return route(at, BROUGHT[kind][i][0])[2][0]
@@ -205,6 +206,9 @@
         for name in first:
             push(name)
         prepare()
+        if kind:
+            sums[...] = jnp.zeros_like(sums)
+            sums[at.me] = sum_tiles(w, at.me, 0, width)
         for n, name in enumerate(order):
             if name[1] == "z":
                 for which, index, to in ((0, n, up), (1, 55 + name[2], down)):
@@ -221,7 +225,10 @@
                 i, q = over[n]
                 got = handed(kind, section(kind, i), q)
                 start(got, got, 70 + 15 * q + i, at.sib)
-                tally(kind, section(kind, i), q)
+                if kind:
+                    tally(section(kind, i), q)
+        if kind:
+            start(sums, sums, 100, at.sib)
         for c in sent:
             c.wait_send()
 
@@ -230,16 +237,12 @@
             sec = section(kind, i)
             got = handed(kind, sec, q)
             remote(got, got, send.at[70 + 15 * q + i], recv.at[70 + 15 * q + i], at.sib).wait_recv()
-            tally(kind, sec, q)
-
-    sums[...] = jnp.zeros_like(sums)
-    for kind in range(2):
-        for q in range(2):
-            tally(kind, at.me, q)
+
     pl.when(at.core == 0)(lambda: run(0, FIRST_A, ORDER_A))
     pl.when(at.core == 1)(lambda: run(1, FIRST_B, ORDER_B))
     pl.when(at.core == 1)(lambda: take(0, ORDER_A))
     pl.when(at.core == 0)(lambda: take(1, ORDER_B))
+    pl.when(at.core == 0)(lambda: remote(sums, sums, send.at[100], recv.at[100], at.sib).wait_recv())
 
 
 def grams(w, rows, raw, gg, mm):
@@ -247,11 +250,12 @@
     tile = lambda b: w[1, b * 8:(b + 1) * 8].reshape(256, width)
 
     def block(kind, _):
+        beside = rows.at[pl.ds(pl.multiple_of((1 - kind) * ROWS, ROWS), 2 * ROWS)]
         for i in range(2):
             lhs = w[kind, i * 8:(i + 1) * 8].reshape(256, width)
             for b in range(i + 1):
                 raw[2 * kind + i, :, b * 256:(b + 1) * 256] = dot(lhs, tile(b), NT)
-            raw[2 * kind + i, :, 512:768] = dot(lhs, rows[...], NT)
+            raw[2 * kind + i, :, 512:768] = dot(lhs, beside[...], NT)
         return 0
 
     lax.fori_loop(0, 2, block, 0)
@@ -272,19 +276,18 @@
             keep(mm, j, s * 128, raw[j // 2, (j % 2) * 128:(j % 2 + 1) * 128, s * 128:(s + 1) * 128].T)
 
 
-def chain(width, stat, row_sums, raw, gg, mm, u, v, c, acts, ds, fs, sc):
+def chain(width, stat, row_sums, wide, raw, gg, mm, u, v, c, acts, ds, fs, sc):
     for i in range(2):
         half = slice(i * 256, (i + 1) * 256)
-        u[half] = raw[i, :, 640:768]
+        u[half] = raw[i, :, 512:640]
         v[half] = raw[2 + i, :, 640:768]
         c[half] = raw[2 + i, :, 512:640]
 
-    for kind in range(2):
-        for s in range(S):
-            row_sums[kind, s] = jnp.broadcast_to(jnp.sum(row_sums[kind, s], axis=1, keepdims=True), (R, ROWS))
+    for s in range(S):
+        wide[s] = jnp.broadcast_to(jnp.sum(row_sums[s], axis=1, keepdims=True), (R, ROWS))
 
     def sums(kind, s):
-        return row_sums[kind, s]
+        return wide[s] if kind else raw[s // 8, (s % 8) * R:(s % 8 + 1) * R, 640:768]
 
     def spot(a, s):
         o = s % 4
@@ -340,28 +343,39 @@
             c[0:j * R] += dot(mm[j // 4, 0:j * R], spot(f16, j)) - dot(gg[(j - 1) // 4, ALL:ALL + j * R], spot(d16, j - 1))
 
 
-def kernel(xd, xu, cd, cu, gain, wa, wb, tot,
-           w, rows, stat, row_sums, raw, gg, mm, u, v, c, acts, ds, fs, sc, half, near, part, pieces, total,
-           send, recv, rs_send, rs_recv, a2a_send, a2a_recv, ag_send, ag_recv, sh_send, sh_recv):
+def kernel(xd, xu, cd, cu, gain, wa, wb, out_ref, gg_out,
+           w, data, rows, stat, row_sums, wide, raw, gg, mm, u, v, c, acts, ds, fs, sc, half, near, part, pieces, beside, merged, total, tot,
+           local, send, recv, rs_send, rs_recv, pr_send, pr_recv, a2a_send, a2a_recv, ag_send, ag_recv, sh_send, sh_recv):
     at = Place()
     me, core, deep = at.me, at.core, at.deep
     width = rows.shape[1]
     step = width // deep
-    far_first = sorted(range(deep), key=lambda d: (-min(d, deep - d), d))
+    hops = lambda d: min(d, deep - d)
+    far_first = sorted(range(deep), key=lambda d: (-hops(d), d))
+    distant = [k for k in range(deep) if hops(far_first[k]) >= max(1, deep * 3 // 8)]
     spots = [(k, e) for k in range(deep) for e in range(2) if (far_first[k], e) != (0, 0)]
-    w[0, me] = (gain[...].astype(F32) * wa[...].astype(F32)).astype(BF16)
-    w[1, me] = wb[...]
-    greet([at.right, at.left, at.cross, at.sib] + [at.spot(far_first[k], e)[2] for k, e in spots])
+    loads = [pltpu.make_async_copy(ref, data.at[i], local.at[i]) for i, ref in enumerate((cd, cu, xd, xu))]
+    for load in loads:
+        load.start()
+
+    def own():
+        w[0, me] = (gain[...].astype(F32) * wa[...].astype(F32)).astype(BF16)
+        w[1, me] = wb[...]
+
+    greet([at.right, at.left, at.cross, at.sib] + [at.spot(far_first[k], e)[2] for k, e in spots], own)
 
     def prepare():
-        for i, ref in enumerate((cd, cu, xd, xu)):
+        for load in loads:
+            load.wait()
+        rows[2 * ROWS:] = jnp.ones((ROWS, width), BF16)
+        for i in range(4):
             for b in range(4):
-                val = jnp.concatenate([ref[2 * b].astype(F32), ref[2 * b + 1].astype(F32)], axis=0)
+                val = jnp.concatenate([data[i, 2 * b].astype(F32), data[i, 2 * b + 1].astype(F32)], axis=0)
                 rows[i * 64 + b * 16:i * 64 + (b + 1) * 16] = val.astype(BF16)
         mus, qs = [], []
-        for ref in (xd, xu):
+        for i in (2, 3):
             for b in range(8):
-                val = ref[b].astype(F32)
+                val = data[i, b].astype(F32)
                 mean = jnp.sum(val, axis=1, keepdims=True) * (1.0 / width)
                 val = val - mean
                 mus.append(mean)
@@ -372,7 +386,7 @@
 
     spread(at, w, row_sums, send, recv, prepare)
     grams(w, rows, raw, gg, mm)
-    chain(width, stat, row_sums, raw, gg, mm, u, v, c, acts, ds, fs, sc)
+    chain(width, stat, row_sums, wide, raw, gg, mm, u, v, c, acts, ds, fs, sc)
 
     at_row = lax.broadcasted_iota(jnp.int32, (ALL, ROWS), 0)
     flat = lambda ref: ref[...].reshape(ALL, ROWS).astype(F32)
@@ -389,7 +403,7 @@
         z = at.spot(far_first[k], 0)[1]
         cols = pl.ds(pl.multiple_of(z * step, step), step)
         from_b = dot(zxd, w[1, :, :, cols].reshape(ALL, step))
-        x = rows[ROWS:, cols].astype(F32) + from_b[0:ROWS]
+        x = rows[ROWS:2 * ROWS, cols].astype(F32) + from_b[0:ROWS]
         dy = rows[0:ROWS, cols].astype(F32) + dot(fd, w[0, :, :, cols].reshape(ALL, step)) - from_b[ROWS:] - cc * x - ee
         half[k, 0:R] = dot(f, (x - mu).astype(BF16)).astype(BF16)
         half[k, R:] = dot(act, dy.astype(BF16)).astype(BF16)
@@ -401,23 +415,48 @@
         y = at.y_lo if e == 0 else 1 - at.y_lo
         return part.at[k, pl.ds(pl.multiple_of(y * H, H), H)]
 
-    out, moved = [], []
+    out, moved, swaps, came = [], [], {}, []
+
+    def give(b, e, src):
+        n = 2 * b + e
+        came.append(remote(src, pieces.at[n], a2a_send.at[n], a2a_recv.at[n], at.spot(far_first[b], e)[2]))
+        came[-1].start()
+
+    def settle(b):
+        out[b].wait_recv()
+        part[b] = (near[b].astype(F32) + half[b, pl.ds(pl.multiple_of(core * R, R), R)].astype(F32)).astype(BF16)
+        if b in distant:
+            n = distant.index(b)
+            swaps[b] = remote(piece(b, 1), beside.at[n], pr_send.at[n], pr_recv.at[n], at.pair)
+            swaps[b].start()
+        else:
+            for e in range(2):
+                if (b, e) in spots:
+                    give(b, e, piece(b, e))
+
+    def forward(b):
+        n = distant.index(b)
+        swaps[b].wait_recv()
+        merged[n] = (beside[n].astype(F32) + piece(b, 0)[...].astype(F32)).astype(BF16)
+        give(b, 0, merged.at[n])
+
+    lag = min(4, deep - 1)
     for k in range(deep + 1):
         if k < deep:
             out.append(block(k))
         if k > 0:
-            b = k - 1
-            out[b].wait_recv()
-            part[b] = (near[b].astype(F32) + half[b, pl.ds(pl.multiple_of(core * R, R), R)].astype(F32)).astype(BF16)
-            for e in range(2):
-                if (b, e) in spots:
-                    n = 2 * b + e
-                    moved.append(remote(piece(b, e), pieces.at[n], a2a_send.at[n], a2a_recv.at[n], at.spot(far_first[b], e)[2]))
-                    moved[-1].start()
+            settle(k - 1)
+        if k - 1 - lag in distant:
+            forward(k - 1 - lag)
+    for b in distant:
+        if b + 1 + lag > deep:
+            forward(b)
     acc = piece(far_first.index(0), 0)[...].astype(F32)
-    for copy, (k, e) in zip(moved, spots):
-        copy.wait_recv()
-        acc = acc + pieces[2 * k + e].astype(F32)
+    order = [(k, e) for k, e in spots if k not in distant] + [(k, 0) for k in distant]
+    for k, e in order:
+        n = 2 * k + e
+        remote(total, pieces.at[n], a2a_send.at[n], a2a_recv.at[n], at.pair).wait_recv()
+        acc = acc + pieces[n].astype(F32)
     total[...] = acc.astype(BF16)
 
     def landing(kind, y, z):
@@ -425,25 +464,42 @@
 
     mine = landing(core, at.y_lo, at.z)
     for k, e in spots:
+        if k not in distant or e == 0:
+            n = 2 * k + e
+            moved.append(remote(total, mine, ag_send.at[n], ag_recv.at[n], at.spot(far_first[k], e)[2]))
+            moved[-1].start()
+    mine[...] = total[...]
+    shared = []
+
+    def share(y, z):
+        got = landing(core, y, z)
+        shared.append((y, z))
+        moved.append(remote(got, got, sh_send.at[len(shared) - 1], sh_recv.at[len(shared) - 1], at.sib))
+        moved[-1].start()
+
+    share(at.y_lo, at.z)
+    order = [(k, 0) for k in distant] + [(k, e) for k, e in reversed(spots) if k not in distant] + [(k, 1) for k in distant]
+    for k, e in order:
         n = 2 * k + e
-        moved.append(remote(total, mine, ag_send.at[n], ag_recv.at[n], at.spot(far_first[k], e)[2]))
-        moved[-1].start()
-    mine[...] = total[...]
-    moved.append(remote(mine, mine, sh_send.at[0], sh_recv.at[0], at.sib))
-    moved[-1].start()
-    came = [(at.y_lo, at.z)]
-    for i, (k, e) in enumerate(spots):
-        n = 2 * k + e
-        y, z, to = at.spot(-far_first[k], e)
+        y, z, _ = at.spot(-far_first[k], e)
         got = landing(core, y, z)
-        came.append((y, z))
-        remote(got, got, ag_send.at[n], ag_recv.at[n], to).wait_recv()
-        moved.append(remote(got, got, sh_send.at[1 + i], sh_recv.at[1 + i], at.sib))
-        moved[-1].start()
-    for i, (y, z) in enumerate(came):
+        remote(got, got, ag_send.at[n], ag_recv.at[n], at.pair).wait_recv()
+        if k in distant and e == 0:
+            moved.append(remote(got, got, ag_send.at[n + 1], ag_recv.at[n + 1], at.pair))
+            moved[-1].start()
+        share(y, z)
+    for i, (y, z) in enumerate(shared):
         got = landing(1 - core, y, z)
         remote(got, got, sh_send.at[i], sh_recv.at[i], at.sib).wait_recv()
-    for copy in out + moved:
+    for i in range(width // ROWS):
+        cols = slice(i * ROWS, (i + 1) * ROWS)
+        h = tot[0, :, cols].astype(F32)
+        out_ref[0:R, cols] = gain[:, cols].astype(F32) * h
+        out_ref[R:, cols] = tot[1, :, cols].astype(F32)
+        product = wa[:, cols].astype(F32) * h
+        gg_out[i:i + 1] = jnp.sum(product[0:H], axis=0, keepdims=True)
+        gg_out[width // ROWS + i:width // ROWS + i + 1] = jnp.sum(product[H:], axis=0, keepdims=True)
+    for copy in out + came + list(swaps.values()) + moved:
         copy.wait_send()
 
 
@@ -453,16 +509,19 @@
     step = width // deep
     vmem = pl.BlockSpec(memory_space=pltpu.VMEM)
     sems = lambda n: [pltpu.SemaphoreType.DMA((n,)), pltpu.SemaphoreType.DMA((n,))]
-    total = pl.pallas_call(
+    far = max(1, len([d for d in range(deep) if min(d, deep - d) >= max(1, deep * 3 // 8)]))
+    total, gg = pl.pallas_call(
         kernel,
-        out_shape=jax.ShapeDtypeStruct((2, R, width), BF16),
-        in_specs=[vmem] * 7,
-        out_specs=vmem,
+        out_shape=(jax.ShapeDtypeStruct((2 * R, width), F32), jax.ShapeDtypeStruct((2 * (width // ROWS), ROWS), F32)),
+        in_specs=[pl.BlockSpec(memory_space=pl.ANY)] * 4 + [vmem] * 3,
+        out_specs=(vmem, vmem),
         scratch_shapes=[
             pltpu.VMEM((2, S, R, width), BF16),
-            pltpu.VMEM((2 * ROWS, width), BF16),
+            pltpu.VMEM((4, 8, 8, width), BF16),
+            pltpu.VMEM((3 * ROWS, width), BF16),
             pltpu.VMEM((8, ROWS), F32),
-            pltpu.VMEM((2, S, R, ROWS), F32),
+            pltpu.VMEM((S, R, ROWS), F32),
+            pltpu.VMEM((S, R, ROWS), F32),
             pltpu.VMEM((4, 256, 768), F32),
             pltpu.VMEM((4, 2 * ALL, 256), BF16),
             pltpu.VMEM((4, ALL, 256), BF16),
@@ -477,13 +536,17 @@
             pltpu.VMEM((deep, R, step), BF16),
             pltpu.VMEM((deep, R, step), BF16),
             pltpu.VMEM((2 * deep, H, step), BF16),
+            pltpu.VMEM((far, H, step), BF16),
+            pltpu.VMEM((far, H, step), BF16),
             pltpu.VMEM((H, step), BF16),
+            pltpu.VMEM((2, R, width), BF16),
+            pltpu.SemaphoreType.DMA((4,)),
         ]
-        + sems(100) + sems(deep) + sems(2 * deep) + sems(2 * deep) + sems(2 * deep),
+        + sems(101) + sems(deep) + sems(far) + sems(2 * deep) + sems(2 * deep) + sems(2 * deep),
         compiler_params=pltpu.CompilerParams(collective_id=0, has_side_effects=True, vmem_limit_bytes=56 * 2**20),
     )(x_down[0], x_up[0], cot_down[0], cot_up[0], gain, w_a[0], w_b[0])
-    h = total[0].astype(F32)
-    return jnp.sum(w_a[0].astype(F32) * h, axis=0)[None], (gain.astype(F32) * h)[None], total[1].astype(F32)[None]
+    gg = lax.optimization_barrier(gg[:width // ROWS] + gg[width // ROWS:])
+    return gg.reshape(1, width), total[:R][None], total[R:][None]
 
 
 def solution(mesh):

time: 94.5 us -> 93.2 us (0.986)
  other arithmetic: 4.28 us -> 1.36 us
  local copies, waits for them, and re-layouts: 0.01 us -> 2.43 us
    broadcast_in_dim x0 -> x1, local copies, waits for them, and re-layouts: none -> 2.43 us  [on_device(): return (gg.reshape(1, width), total[:R][None], total[R:][None])]
    reduce_sum x1 -> x0, other arithmetic: 1.76 us -> none  [on_device(): jnp.sum(w_a[0].astype(F32) * h, axis=0)[None]]
    mul x2 -> x0, other arithmetic: 1.64 us -> none  [on_device(): gain.astype(F32) * h]
    add x0 -> x1, other arithmetic: none -> 1.36 us  [on_device(): gg = lax.optimization_barrier(gg[:width // ROWS] + gg[width // ROWS:])]
where the time goes in v4:
time: 93.2 us; the launch traced here: 93 us
  Pallas kernels  88.5 us (95%)
  local copies, waits for them, and re-layouts  2.43 us (3%)
  other arithmetic  1.36 us (1%)
    pallas_call x1, Pallas kernels, on_device(): pl.pallas_call(kernel, out_shape=(jax.ShapeDtypeStruct((2 * R, width), F3...  88.5 us
    broadcast_in_dim x1, local copies, waits for them, and re-layouts, on_device(): return (gg.reshape(1, width), total[:R][None], total[R:][None])  2.43 us

profile of v4, /device:TPU:1, one launch (start us, length us, event | category | flops | bytes accessed | tf_op | source)
XLA Modules:
  0.0 93.0 jit_solution(9962283801272331594)
XLA Ops:
  0.6 88.5 %shard_map.94 = (f32[64,5120]{1,0:T(8,128)}, f32[80,128]{1,0:T(8,128)}) custom-call(bf16[8,8,5120]{2,1,0:T(8,128)(2,1)} %bitcast.11, bf16[8,8,5120]{2,1,0:T(8,128)(2,1)} %bitcast.12, bf16[8,8,5120]{2,1,0:T(8,128)(2,1)} %bitcast.13, bf16[8,8,5120]{2,1,0:T(8,128)(2,1)} %bitcast.14, bf16[1,5120]{1,0:T(2,128)(2,1)} %gain.1, bf16[32,5120]{1,0:T(8,128)(2,1)} %bitcast.15, ...), custom_call_target="tpu_custom_call" | custom-call | tf_op jit(solution)/shard_map/pallas_call | solution.py:513
  89.2 1.4 %slice_add_fusion = f32[40,128]{1,0:T(8,128)} fusion(f32[80,128]{1,0:T(8,128)} %get-tuple-element.5), kind=kLoop, calls=%fused_computation.2 | loop fusion | flops 5120 | bytes 61440 | tf_op jit(solution)/shard_map/add | solution.py:548
  90.5 2.4 %slice_bitcast_fusion = (f32[1,32,5120]{2,1,0:T(8,128)}, f32[1,32,5120]{2,1,0:T(8,128)}) fusion(f32[64,5120]{1,0:T(8,128)} %get-tuple-element.6), kind=kLoop, calls=%fused_computation | loop fusion | bytes 2621440 | tf_op jit(solution)/shard_map/broadcast_in_dim | solution.py:549
